TPU v7x, 32 devices: a whole 2x2x4 slice. The times are simulated.
32 devices in a mesh: dp: 8 (over z, y), layer: 4 (over x, core).
Axes of the slice: x: 2, y: 2, z: 4, core: 2. Of those that a mesh axis runs over, the one named last changes fastest.
Arguments:
- inputs: bfloat16 [32768, 640], P(('dp', 'layer')), may hold values from -6 to 6
- encoder_out: bfloat16 [4, 32768, 640], P('layer', 'dp'), may hold values from -6 to 6
- query_self: bfloat16 [640, 640], replicated, may hold values from -0.25 to 0.25
- key_self: bfloat16 [640, 640], replicated, may hold values from -0.25 to 0.25
- value_self: bfloat16 [640, 640], replicated, may hold values from -0.25 to 0.25
- out_self: bfloat16 [640, 640], replicated, may hold values from -0.5 to 0.5
- query_cross: bfloat16 [640, 640], replicated, may hold values from -0.25 to 0.25
- key_cross: bfloat16 [640, 640], replicated, may hold values from -0.25 to 0.25
- value_cross: bfloat16 [640, 640], replicated, may hold values from -0.25 to 0.25
- out_cross: bfloat16 [640, 640], replicated, may hold values from -0.5 to 0.5
- feed_up: bfloat16 [640, 3072], replicated, may hold values from -0.25 to 0.25
- feed_down: bfloat16 [3072, 640], replicated, may hold values from -0.15625 to 0.15625
- gain_self: float32 [640], replicated, may hold values from 0.25 to 1.75
- gain_cross: float32 [640], replicated, may hold values from 0.25 to 1.75
- gain_feed: float32 [640], replicated, may hold values from 0.25 to 1.75
- seg_target: int32 [128, 256], P(('dp', 'layer')), may hold values from 0 to 7, never falling along the last dimension, each value on 1 to 64 neighbouring positions
- seg_source: int32 [128, 256], P(('dp', 'layer')), may hold values from 0 to 7, never falling along the last dimension, each value on 1 to 64 neighbouring positions
- subnet_of_row: int32 [128], P('dp'), may hold values from 0 to 5
- chosen_layers: int32 [6, 2], replicated, may hold values from 0 to 3, all different within a row
- out_grad: bfloat16 [32768, 640], P(('dp', 'layer')), may hold values from -6 to 6
Outputs:
- layer_out: bfloat16 [32768, 640], P(('dp', 'layer'))
- input_grad: bfloat16 [32768, 640], P(('dp', 'layer'))
- encoder_grad: float32 [4, 32768, 640], P('layer', 'dp')
- grad_query_self: float32 [640, 640], P('dp')
- grad_key_self: float32 [640, 640], P('dp')
- grad_value_self: float32 [640, 640], P('dp')
- grad_out_self: float32 [640, 640], P('dp')
- grad_query_cross: float32 [640, 640], P('dp')
- grad_key_cross: float32 [640, 640], P('dp')
- grad_value_cross: float32 [640, 640], P('dp')
- grad_out_cross: float32 [640, 640], P('dp')
- grad_feed_up: float32 [640, 3072], P('dp')
- grad_feed_down: float32 [3072, 640], P('dp')
- grad_gain_self: float32 [640], P('dp')
- grad_gain_cross: float32 [640], P('dp')
- grad_gain_feed: float32 [640], P('dp')
Inputs may be any that keep to these rules, and one draw needn't show every extreme that they name: `seg_target`: each row holds 8 sentences numbered in order, each of 1 to 64 tokens, one of exactly 64. `seg_source`: each row holds 8 sentences numbered in order, each of 1 to 64 tokens, one of exactly 64. `chosen_layers`: each sub-net names 2 different encoder layers; every layer is named by some sub-net.
All inputs are finite; a program needn't handle non-finite values.
Results may differ from a plain program's by a relative error of at most 0.018.
Values may be sent and summed in bfloat16 or wider, within the bound.
No kernel may reach another device: no remote copies, remote signals or barrier semaphores. Data moves between devices by JAX's collectives and lax.ppermute only.
A program may use at most 192 MiB of HBM per device.

v0:
```python
import math

import jax
import jax.numpy as jnp
from jax import lax
from jax.sharding import PartitionSpec as P

HEADS = 8
HEAD = 80
ROW_LEN = 256


def to_low(value):
    return value.astype(jnp.bfloat16)


def dense(left, right):
    return jnp.dot(left, right, preferred_element_type=jnp.float32)


def dense_back(grad, weight):
    return lax.dot_general(
        grad, weight, (((1,), (1,)), ((), ())), preferred_element_type=jnp.float32
    )


def weight_grad(inputs, grad):
    return lax.dot_general(
        inputs, grad, (((0,), (0,)), ((), ())), preferred_element_type=jnp.float32
    )


def norm_forward(value, gain):
    centred = value - jnp.mean(value, axis=-1, keepdims=True)
    inverse = lax.rsqrt(jnp.mean(centred * centred, axis=-1, keepdims=True) + 1e-05)
    normed = centred * inverse
    return (normed * gain, normed, inverse)


def norm_backward(grad, gain, normed, inverse):
    gain_grad = jnp.sum(grad * normed, axis=0)
    scaled = grad * gain
    inner = (
        scaled
        - jnp.mean(scaled, axis=-1, keepdims=True)
        - normed * jnp.mean(scaled * normed, axis=-1, keepdims=True)
    )
    return (inner * inverse, gain_grad)


def masked_scores(queries, key_block, allowed):
    scores = jnp.einsum(
        "rqhe,rkhe->rhqk", queries, key_block, preferred_element_type=jnp.float32
    ) * (1.0 / math.sqrt(HEAD))
    return jnp.where(allowed[:, None], scores, -1000000000.0)


def attend_forward(queries, key_block, value_block, allowed):
    scores = masked_scores(queries, key_block, allowed)
    row_peak = jnp.max(scores, axis=-1, keepdims=True)
    raised = jnp.exp(scores - row_peak)
    denominator = jnp.sum(raised, axis=-1, keepdims=True)
    weights = to_low(raised / denominator)
    result = to_low(
        jnp.einsum("rhqk,rkhe->rqhe", weights, value_block, preferred_element_type=jnp.float32)
    )
    return (result, row_peak + jnp.log(denominator))


def attend_backward(result_grad, queries, key_block, value_block, allowed, log_total):
    scores = masked_scores(queries, key_block, allowed)
    probs = jnp.exp(scores - log_total)
    prob_grad = jnp.einsum(
        "rqhe,rkhe->rhqk", result_grad, value_block, preferred_element_type=jnp.float32
    )
    value_grad = jnp.einsum(
        "rhqk,rqhe->rkhe", to_low(probs), result_grad, preferred_element_type=jnp.float32
    )
    row_delta = jnp.sum(prob_grad * probs, axis=-1, keepdims=True)
    score_grad = to_low(probs * (prob_grad - row_delta))
    scale_factor = 1.0 / math.sqrt(HEAD)
    query_grad = (
        jnp.einsum("rhqk,rkhe->rqhe", score_grad, key_block, preferred_element_type=jnp.float32)
        * scale_factor
    )
    key_grad = (
        jnp.einsum("rhqk,rqhe->rkhe", score_grad, queries, preferred_element_type=jnp.float32)
        * scale_factor
    )
    return (to_low(query_grad), to_low(key_grad), to_low(value_grad))


def on_device(
    inputs,
    encoder_out,
    query_self,
    key_self,
    value_self,
    out_self,
    query_cross,
    key_cross,
    value_cross,
    out_cross,
    feed_up,
    feed_down,
    gain_self,
    gain_cross,
    gain_feed,
    seg_target,
    seg_source,
    subnet_of_row,
    chosen_layers,
    out_grad,
):
    arrived = lax.all_to_all(encoder_out, "layer", split_axis=1, concat_axis=0, tiled=True)
    tok_count = inputs.shape[0]
    width = inputs.shape[1]
    row_count = tok_count // ROW_LEN
    layer_count = lax.axis_size("layer")
    own_layer = lax.axis_index("layer")

    def split_heads(flat):
        return flat.reshape(row_count, ROW_LEN, HEADS, HEAD)

    def flatten(heads_form):
        return heads_form.reshape(tok_count, width)

    positions = jnp.arange(ROW_LEN)
    causal = positions[:, None] >= positions[None, :]
    self_mask = (seg_target[:, :, None] == seg_target[:, None, :]) & causal[None]
    cross_mask = seg_target[:, :, None] == seg_source[:, None, :]
    picked = jnp.sum(
        (chosen_layers[:, :, None] == jnp.arange(layer_count)[None, None, :]).astype(jnp.float32),
        axis=1,
    )
    row_pick = (subnet_of_row[:, None] == jnp.arange(chosen_layers.shape[0])[None, :]).astype(
        jnp.float32
    )
    block_hits = jnp.dot(row_pick, picked)
    my_hits = lax.dynamic_slice_in_dim(block_hits, own_layer * row_count, row_count, 0)
    inputs_full = inputs.astype(jnp.float32)
    normed_value, plain_self, inverse_self = norm_forward(inputs_full, gain_self)
    normed_self = to_low(normed_value)
    queries_self = to_low(dense(normed_self, query_self))
    keys_self = to_low(dense(normed_self, key_self))
    values_self = to_low(dense(normed_self, value_self))
    attn_heads, lse_self = attend_forward(
        split_heads(queries_self), split_heads(keys_self), split_heads(values_self), self_mask
    )
    attn_self = flatten(attn_heads)
    after_self = inputs_full + dense(attn_self, out_self)
    normed_value, plain_cross, inverse_cross = norm_forward(after_self, gain_cross)
    normed_cross = to_low(normed_value)
    queries_cross = to_low(dense(normed_cross, query_cross))
    layered = arrived.reshape(layer_count, row_count, ROW_LEN, width)
    memory_full = 0.5 * jnp.einsum(
        "re,erld->rld", to_low(my_hits), layered, preferred_element_type=jnp.float32
    )
    memory = to_low(memory_full.reshape(tok_count, width))
    keys_cross = to_low(dense(memory, key_cross))
    values_cross = to_low(dense(memory, value_cross))
    attn_heads, lse_cross = attend_forward(
        split_heads(queries_cross), split_heads(keys_cross), split_heads(values_cross), cross_mask
    )
    attn_cross = flatten(attn_heads)
    after_cross = after_self + dense(attn_cross, out_cross)
    normed_value, plain_feed, inverse_feed = norm_forward(after_cross, gain_feed)
    normed_feed = to_low(normed_value)
    hidden_pre = dense(normed_feed, feed_up)
    hidden = to_low(jax.nn.gelu(hidden_pre))
    layer_out = to_low(after_cross + dense(hidden, feed_down))
    grad_top = out_grad.astype(jnp.float32)
    down_in = to_low(grad_top)
    grad_down = weight_grad(hidden, down_in)
    hidden_grad = dense_back(down_in, feed_down)
    unused_value, gelu_pull = jax.vjp(jax.nn.gelu, hidden_pre)
    pre_grad = to_low(gelu_pull(hidden_grad)[0])
    grad_up = weight_grad(normed_feed, pre_grad)
    back_feed, grad_gain_feed = norm_backward(
        dense_back(pre_grad, feed_up), gain_feed, plain_feed, inverse_feed
    )
    grad_after_cross = grad_top + back_feed
    cross_in = to_low(grad_after_cross)
    grad_out_cross = weight_grad(attn_cross, cross_in)
    attn_grad = to_low(dense_back(cross_in, out_cross))
    query_grad, key_grad, value_grad = attend_backward(
        split_heads(attn_grad),
        split_heads(queries_cross),
        split_heads(keys_cross),
        split_heads(values_cross),
        cross_mask,
        lse_cross,
    )
    query_grad = flatten(query_grad)
    key_grad = flatten(key_grad)
    value_grad = flatten(value_grad)
    grad_query_cross = weight_grad(normed_cross, query_grad)
    grad_key_cross = weight_grad(memory, key_grad)
    grad_value_cross = weight_grad(memory, value_grad)
    memory_grad = to_low(dense_back(key_grad, key_cross) + dense_back(value_grad, value_cross))
    returned = lax.all_gather(memory_grad, "layer", axis=0, tiled=True)
    own_hits = jnp.sum(
        block_hits * (jnp.arange(layer_count) == own_layer)[None, :].astype(jnp.float32), axis=1
    )
    encoder_grad = (0.5 * own_hits[:, None, None] * returned.reshape(-1, ROW_LEN, width)).reshape(
        encoder_out.shape
    )
    back_cross, grad_gain_cross = norm_backward(
        dense_back(query_grad, query_cross), gain_cross, plain_cross, inverse_cross
    )
    grad_after_self = grad_after_cross + back_cross
    self_in = to_low(grad_after_self)
    grad_out_self = weight_grad(attn_self, self_in)
    attn_grad = to_low(dense_back(self_in, out_self))
    query_grad, key_grad, value_grad = attend_backward(
        split_heads(attn_grad),
        split_heads(queries_self),
        split_heads(keys_self),
        split_heads(values_self),
        self_mask,
        lse_self,
    )
    query_grad = flatten(query_grad)
    key_grad = flatten(key_grad)
    value_grad = flatten(value_grad)
    grad_query_self = weight_grad(normed_self, query_grad)
    grad_key_self = weight_grad(normed_self, key_grad)
    grad_value_self = weight_grad(normed_self, value_grad)
    norm_in = (
        dense_back(query_grad, query_self)
        + dense_back(key_grad, key_self)
        + dense_back(value_grad, value_self)
    )
    back_self, grad_gain_self = norm_backward(norm_in, gain_self, plain_self, inverse_self)
    input_grad = to_low(grad_after_self + back_self)
    summed = (
        lax.psum_scatter(grad_query_self, "dp", scatter_dimension=0, tiled=True),
        lax.psum_scatter(grad_key_self, "dp", scatter_dimension=0, tiled=True),
        lax.psum_scatter(grad_value_self, "dp", scatter_dimension=0, tiled=True),
        lax.psum_scatter(grad_out_self, "dp", scatter_dimension=0, tiled=True),
        lax.psum_scatter(grad_query_cross, "dp", scatter_dimension=0, tiled=True),
        lax.psum_scatter(grad_key_cross, "dp", scatter_dimension=0, tiled=True),
        lax.psum_scatter(grad_value_cross, "dp", scatter_dimension=0, tiled=True),
        lax.psum_scatter(grad_out_cross, "dp", scatter_dimension=0, tiled=True),
        lax.psum_scatter(grad_up, "dp", scatter_dimension=0, tiled=True),
        lax.psum_scatter(grad_down, "dp", scatter_dimension=0, tiled=True),
        lax.psum_scatter(grad_gain_self, "dp", scatter_dimension=0, tiled=True),
        lax.psum_scatter(grad_gain_cross, "dp", scatter_dimension=0, tiled=True),
        lax.psum_scatter(grad_gain_feed, "dp", scatter_dimension=0, tiled=True),
    )
    summed = (
        lax.psum(summed[0].astype(jnp.bfloat16), "layer").astype(jnp.float32),
        lax.psum(summed[1].astype(jnp.bfloat16), "layer").astype(jnp.float32),
        lax.psum(summed[2].astype(jnp.bfloat16), "layer").astype(jnp.float32),
        lax.psum(summed[3].astype(jnp.bfloat16), "layer").astype(jnp.float32),
        lax.psum(summed[4].astype(jnp.bfloat16), "layer").astype(jnp.float32),
        lax.psum(summed[5].astype(jnp.bfloat16), "layer").astype(jnp.float32),
        lax.psum(summed[6].astype(jnp.bfloat16), "layer").astype(jnp.float32),
        lax.psum(summed[7].astype(jnp.bfloat16), "layer").astype(jnp.float32),
        lax.psum(summed[8].astype(jnp.bfloat16), "layer").astype(jnp.float32),
        lax.psum(summed[9].astype(jnp.bfloat16), "layer").astype(jnp.float32),
        lax.psum(summed[10].astype(jnp.bfloat16), "layer").astype(jnp.float32),
        lax.psum(summed[11].astype(jnp.bfloat16), "layer").astype(jnp.float32),
        lax.psum(summed[12].astype(jnp.bfloat16), "layer").astype(jnp.float32),
    )
    return (
        layer_out,
        input_grad,
        encoder_grad,
        summed[0],
        summed[1],
        summed[2],
        summed[3],
        summed[4],
        summed[5],
        summed[6],
        summed[7],
        summed[8],
        summed[9],
        summed[10],
        summed[11],
        summed[12],
    )


def solution(mesh):
    in_specs = (
        P(("dp", "layer"), None),
        P("layer", "dp", None),
        P(),
        P(),
        P(),
        P(),
        P(),
        P(),
        P(),
        P(),
        P(),
        P(),
        P(),
        P(),
        P(),
        P(("dp", "layer"), None),
        P(("dp", "layer"), None),
        P("dp"),
        P(),
        P(("dp", "layer"), None),
    )
    out_specs = (
        P(("dp", "layer"), None),
        P(("dp", "layer"), None),
        P("layer", "dp", None),
        P("dp", None),
        P("dp", None),
        P("dp", None),
        P("dp", None),
        P("dp", None),
        P("dp", None),
        P("dp", None),
        P("dp", None),
        P("dp", None),
        P("dp", None),
        P("dp"),
        P("dp"),
        P("dp"),
    )
    return jax.shard_map(
        on_device, mesh=mesh, in_specs=in_specs, out_specs=out_specs, check_vma=False
    )
```

profile of v0, /device:TPU:0, one launch (start us, length us, event | category | flops | bytes accessed | tf_op | source)
XLA Modules:
  0.0 1194.8 jit_solution(13316268970148171678)
XLA Ops:
  8.0 10.5 copy.294
  19.0 112.9 %reduce = bf16[4096,640]{1,0:T(8,128)(2,1)} reduce(bf16[4096,1,640]{2,1,0:T(2,128)(2,1)} %bitcast.140, bf16[]{:T(256)} %broadcast.218), dimensions={1}, to_apply=%bitcast.139.reduce_sub_computation | reduce | bytes 10485762
  131.9 5.8 reshape.248
  137.7 5.2 all-to-all-start
  147.9 3.1 reshape.242
  151.0 3.0 copy.211
  154.0 4.2 convolution_convert_fusion.6
  158.2 4.6 reshape.241
  162.8 4.1 copy.210
  167.0 3.7 convolution_convert_fusion.7
  170.6 4.6 reshape.240
  175.2 4.2 copy.212
  179.4 2.5 copy.225
  183.3 3.0 fusion.78
  196.9 3.1 reshape.244
  200.1 3.0 copy.219
  203.1 9.5 reshape.249
  212.7 7.2 copy.280
  219.8 6.6 fusion.11
  229.2 3.1 reshape.245
  232.3 3.0 copy.220
  235.3 4.4 convolution_convert_fusion.4
  239.7 4.6 reshape.243
  244.3 4.3 copy.221
  248.7 2.6 fusion.80
  260.4 8.3 fusion.67
  268.7 13.5 %fusion.6 = bf16[1024,3072]{1,0:T(8,128)(2,1)S(1)} fusion(f32[1024,3072]{1,0:T(8,128)} %fusion.67, bf16[1024,640]{1,0:T(8,128)(2,1)S(1)} %copy-done.30, bf16[3072,640]{1,0:T(8,128)(2,1)S(1)} %copy-done.64), kind=kOutput, calls=%fused_computation.8 | convolution fusion | flops 4089446400 | bytes 24117248 | tf_op jit(solution)/shard_map/dot_general | solution.py:22
  282.3 5.2 multiply_reduce_fusion.2
  292.3 4.4 convolution_convert_fusion.1
  296.7 5.0 reshape.246
  301.7 4.2 copy.227
  306.7 5.3 fusion.47
  316.9 6.3 multiply_reduce_fusion.1
  323.2 4.6 multiply_convert_fusion.2
  334.9 3.5 fusion.50
  343.3 4.5 multiply_reduce_fusion.3
  352.6 4.4 convolution_convert_fusion
  357.1 4.6 reshape.247
  361.7 4.1 copy.233
  365.8 5.2 fusion.44
  376.2 6.3 multiply_reduce_fusion
  382.5 4.7 multiply_convert_fusion.1
  391.6 2.5 fusion.71
  394.2 3.5 fusion.51
  400.1 2.5 fusion.73
  403.1 11.9 %fusion.68 = f32[3072,640]{1,0:T(8,128)} fusion(bf16[1024,640]{1,0:T(8,128)(2,1)} %param.39, f32[1024,3072]{1,0:T(8,128)} %fusion.67), kind=kOutput, calls=%fused_computation.137 | convolution fusion | flops 4054843392 | bytes 21757952 | tf_op jit(solution)/shard_map/dot_general | solution.py:28
  415.7 9.4 fusion.66
  425.2 3.1 fusion.82
  432.4 10.5 add_convert_fusion.1
  442.9 2.7 copy.250
  445.7 2.9 fusion.86
  450.6 3.2 fusion.33
  453.8 38.8 %all-reduce.3 = (bf16[640]{0:T(1024)(128)(2,1)S(1)}, bf16[640]{0:T(1024)(128)(2,1)S(1)}, bf16[640]{0:T(1024)(128)(2,1)S(1)}) all-reduce(f32[640]{0:T(1024)S(1)} %get-tuple-element.100, f32[640]{0:T(1024)S(1)} %copy-done.61, f32[640]{0:T(1024)S(1)} %copy-done.60), channel_id=12, replica_groups=mesh['dp'=8,'layer'=4] {'dp'}, use_global_device_ids=true, to_apply=%region_41.42.clone | all-reduce | flops 1920 | bytes 11520
  492.8 6.0 all-reduce.4
  500.4 3.4 fusion.32
  510.0 55.5 %reduce-scatter.19.cloned.1.call-done = f32[80,640]{1,0:T(8,128)} async-done(((f32[640,640]{1,0:T(8,128)}), f32[80,640]{1,0:T(8,128)}) %reduce-scatter.19.cloned.1.call-update) | async-done | bytes 204816 | tf_op jit(solution)/shard_map/reduce_scatter | solution.py:241
  567.0 66.1 %reduce-scatter.17.cloned.1.call-done = f32[80,640]{1,0:T(8,128)} async-done(((f32[640,640]{1,0:T(8,128)}), f32[80,640]{1,0:T(8,128)}) %reduce-scatter.17.cloned.1.call-update) | async-done | bytes 204816 | tf_op jit(solution)/shard_map/reduce_scatter | solution.py:240
  634.7 66.5 %reduce-scatter.15.cloned.1.call-done = f32[80,640]{1,0:T(8,128)} async-done(((f32[640,640]{1,0:T(8,128)}), f32[80,640]{1,0:T(8,128)}) %reduce-scatter.15.cloned.1.call-update) | async-done | bytes 204816 | tf_op jit(solution)/shard_map/reduce_scatter | solution.py:239
  702.7 66.1 %reduce-scatter.13.cloned.1.call-done = f32[80,640]{1,0:T(8,128)} async-done(((f32[640,640]{1,0:T(8,128)}), f32[80,640]{1,0:T(8,128)}) %reduce-scatter.13.cloned.1.call-update) | async-done | bytes 204816 | tf_op jit(solution)/shard_map/reduce_scatter | solution.py:238
  770.5 66.6 %reduce-scatter.11.cloned.1.call-done = f32[80,640]{1,0:T(8,128)} async-done(((f32[640,640]{1,0:T(8,128)}), f32[80,640]{1,0:T(8,128)}) %reduce-scatter.11.cloned.1.call-update) | async-done | bytes 204816 | tf_op jit(solution)/shard_map/reduce_scatter | solution.py:237
  838.6 141.0 %reduce-scatter.29.cloned.1.call-done = f32[384,640]{1,0:T(8,128)} async-done(((f32[3072,640]{1,0:T(8,128)}), f32[384,640]{1,0:T(8,128)}) %reduce-scatter.29.cloned.1.call-update) | async-done | bytes 983056 | tf_op jit(solution)/shard_map/reduce_scatter | solution.py:246
  981.7 141.2 %reduce-scatter.27.cloned.1.call-done = f32[80,3072]{1,0:T(8,128)} async-done(((f32[640,3072]{1,0:T(8,128)}), f32[80,3072]{1,0:T(8,128)}) %reduce-scatter.27.cloned.1.call-update) | async-done | bytes 983056 | tf_op jit(solution)/shard_map/reduce_scatter | solution.py:245
  1125.0 7.5 multiply_bitcast_fusion
  1132.4 39.9 %all-reduce.8.cloned.1.call-done = (bf16[80,640]{1,0:T(8,128)(2,1)}, bf16[80,640]{1,0:T(8,128)(2,1)}, bf16[80,640]{1,0:T(8,128)(2,1)}, bf16[80,640]{1,0:T(8,128)...) async-done(((bf16[80,640]{1,0:T(8,128)(2,1)}, ...) | async-done | bytes 1802256 | tf_op jit(solution)/shard_map/psum | solution.py:252
  (272 shorter events, 109.5 us)
Async XLA Ops:
  8.0 187.4 %copy-start = (bf16[640,640]{1,0:T(8,128)(2,1)S(1)}, bf16[640,640]{1,0:T(8,128)(2,1)}, u32[]{:S(2)}) copy-start(bf16[640,640]{1,0:T(8,128)(2,1)} %param.26) | copy-start | bytes 2457604
  137.7 5.5 copy-start.62
  137.7 5.5 copy-start.70
  137.7 6.4 copy-start.29
  137.7 65.4 %all-to-all-start = ((bf16[4,2,327680]{2,1,0:T(2,128)(2,1)}), bf16[4,2,327680]{2,1,0:T(2,128)(2,1)}, u32[]{:S(2)}, u32[]{:S(2)}) async-start(bf16[4,2,327680]{2,1,0:T(2,128)(2,1)} %reshape.248), calls=%async_computation | async-start | bytes 10485760 | tf_op jit(solution)/shard_map/all_to_all | solution.py:115
  142.9 362.3 %reduce-scatter.25.cloned.1.call-start = ((), (), s32[]{:S(2)}) async-start(), calls=%async_computation.19 | async-start | bytes 1843200 | tf_op jit(solution)/shard_map/reduce_scatter | solution.py:244
  144.8 47.7 %copy-start.9 = (bf16[1024,640]{0,1:T(8,128)(2,1)}, bf16[1024,640]{0,1:T(8,128)(2,1)S(1)}, u32[]{:S(2)}) copy-start(bf16[1024,640]{0,1:T(8,128)(2,1)S(1)} %copy.206) | copy-start | bytes 3932164
  145.0 21.9 %copy-start.48 = (f32[1024]{0:T(1024)}, f32[1024]{0:T(1024)S(1)}, u32[]{:S(2)}) copy-start(f32[1024]{0:T(1024)S(1)} %broadcast_multiply_fusion.8) | copy-start | bytes 12292
  146.4 20.6 %copy-start.50 = (f32[1024]{0:T(1024)}, f32[1024]{0:T(1024)S(1)}, u32[]{:S(2)}) copy-start(f32[1024]{0:T(1024)S(1)} %add_rsqrt_fusion.2) | copy-start | bytes 12292
  154.0 29.2 %copy-start.17 = (bf16[4,256,8,80]{1,3,2,0:T(8,128)(2,1)}, bf16[4,256,8,80]{1,3,2,0:T(8,128)(2,1)S(1)}, u32[]{:S(2)}) copy-start(bf16[4,256,8,80]{1,3,2,0:T(8,128)(2,1)S(1)} %copy.211) | copy-start | bytes 3932164
  175.2 6.7 copy-start.54
  175.2 6.7 copy-start.55
  186.2 3.3 copy-start.1
  186.3 3.2 copy-start.22
  203.1 45.6 %copy-start.19 = (bf16[4,256,8,80]{1,3,2,0:T(8,128)(2,1)}, bf16[4,256,8,80]{1,3,2,0:T(8,128)(2,1)S(1)}, u32[]{:S(2)}) copy-start(bf16[4,256,8,80]{1,3,2,0:T(8,128)(2,1)S(1)} %copy.219) | copy-start | bytes 3932164
  235.3 13.4 %copy-start.21 = (bf16[4,256,8,80]{1,3,2,0:T(8,128)(2,1)}, bf16[4,256,8,80]{1,3,2,0:T(8,128)(2,1)S(1)}, u32[]{:S(2)}) copy-start(bf16[4,256,8,80]{1,3,2,0:T(8,128)(2,1)S(1)} %copy.220) | copy-start | bytes 3932164
  251.3 3.4 copy-start.2
  251.3 3.4 copy-start.23
  256.3 1.9 copy-start.41
  258.2 2.1 copy-start.63
  260.4 8.3 copy-start.30
  260.4 8.3 copy-start.64
  282.3 5.2 copy-start.73
  282.3 5.2 copy-start.28
  292.3 214.5 %reduce-scatter.23.cloned.1.call-start = ((), (), s32[]{:S(2)}) async-start(), calls=%async_computation.18 | async-start | bytes 1843200 | tf_op jit(solution)/shard_map/reduce_scatter | solution.py:243
  312.0 2.4 copy-start.39
  316.8 191.6 %reduce-scatter.21.cloned.1.call-start = ((), (), s32[]{:S(2)}) async-start(), calls=%async_computation.17 | async-start | bytes 1843200 | tf_op jit(solution)/shard_map/reduce_scatter | solution.py:242
  323.2 4.6 copy-start.20
  327.8 2.0 copy-start.3
  329.8 2.4 copy-start.40
  334.7 230.8 %reduce-scatter.19.cloned.1.call-start = ((), (), s32[]{:S(2)}) async-start(), calls=%async_computation.16 | async-start | bytes 1843200 | tf_op jit(solution)/shard_map/reduce_scatter | solution.py:241
  338.4 2.4 copy-start.7
  338.4 2.4 copy-start.57
  343.2 289.9 %reduce-scatter.17.cloned.1.call-start = ((), (), s32[]{:S(2)}) async-start(), calls=%async_computation.15 | async-start | bytes 1843200 | tf_op jit(solution)/shard_map/reduce_scatter | solution.py:240
  343.3 4.5 copy-start.8
  343.3 4.5 copy-start.16
  347.8 2.4 copy-start.27
  350.2 2.5 copy-start.46
  352.6 348.6 %reduce-scatter.15.cloned.1.call-start = ((), (), s32[]{:S(2)}) async-start(), calls=%async_computation.14 | async-start | bytes 1843200 | tf_op jit(solution)/shard_map/reduce_scatter | solution.py:239
  371.0 2.4 copy-start.10
  371.0 2.4 copy-start.49
  371.0 2.4 copy-start.51
  371.0 2.4 copy-start.53
  375.9 393.0 %reduce-scatter.13.cloned.1.call-start = ((), (), s32[]{:S(2)}) async-start(), calls=%async_computation.13 | async-start | bytes 1843200 | tf_op jit(solution)/shard_map/reduce_scatter | solution.py:238
  382.5 4.7 copy-start.18
  387.2 2.0 copy-start.4
  389.2 2.4 copy-start.11
  394.1 442.9 %reduce-scatter.11.cloned.1.call-start = ((), (), s32[]{:S(2)}) async-start(), calls=%async_computation.12 | async-start | bytes 1843200 | tf_op jit(solution)/shard_map/reduce_scatter | solution.py:237
  397.7 2.4 copy-start.12
  402.6 577.0 %reduce-scatter.29.cloned.1.call-start = ((), (), s32[]{:S(2)}) async-start(), calls=%async_computation.21 | async-start | bytes 8847360 | tf_op jit(solution)/shard_map/reduce_scatter | solution.py:246
  415.1 707.8 %reduce-scatter.27.cloned.1.call-start = ((), (), s32[]{:S(2)}) async-start(), calls=%async_computation.20 | async-start | bytes 8847360 | tf_op jit(solution)/shard_map/reduce_scatter | solution.py:245
  425.1 699.8 %all-gather.2.cloned.1.call-start = ((), (), s32[]{:S(2)}) async-start(), calls=%async_computation.11 | async-start | bytes 6553600 | tf_op jit(solution)/shard_map/all_gather | solution.py:201
  425.2 3.1 copy-start.32
  425.2 3.1 copy-start.67
  428.3 2.7 copy-start.72
  428.3 2.8 copy-start.71
  430.8 741.5 %all-reduce.8.cloned.1.call-start = ((), (), s32[]{:S(2)}) async-start(), calls=%async_computation.22 | async-start | bytes 3604480 | tf_op jit(solution)/shard_map/psum | solution.py:252
  445.7 2.9 copy-start.36
  445.7 2.9 copy-start.69
  448.6 2.0 copy-start.42
  450.6 3.2 copy-start.60
  450.6 3.2 copy-start.61
  1172.3 12.8 %copy-start.44 = (bf16[80,3072]{1,0:T(8,128)(2,1)S(1)}, bf16[80,3072]{1,0:T(8,128)(2,1)}, u32[]{:S(2)}) copy-start(bf16[80,3072]{1,0:T(8,128)(2,1)} %get-tuple-element.119) | copy-start | bytes 1474564
  1172.3 13.8 %copy-start.43 = (bf16[384,640]{1,0:T(8,128)(2,1)S(1)}, bf16[384,640]{1,0:T(8,128)(2,1)}, u32[]{:S(2)}) copy-start(bf16[384,640]{1,0:T(8,128)(2,1)} %get-tuple-element.120) | copy-start | bytes 1474564
  (23 other events, 30.5 us)
Sparse Core Ops, SparseCore 0:
  292.4 68.6 reduce-scatter.24
  364.9 64.3 reduce-scatter.22
  432.8 64.4 reduce-scatter.20
  501.0 64.4 reduce-scatter.18
  568.7 64.3 reduce-scatter.16
  636.8 64.3 reduce-scatter.14
  704.6 64.2 reduce-scatter.12
  772.7 64.2 reduce-scatter.10
  840.7 138.9 reduce-scatter.28
  983.7 139.0 reduce-scatter.26
Sparse Core Ops, SparseCore 1:
  430.9 43.5 all-gather.1
  1125.0 47.3 all-reduce.7
where the time goes:
time: 1200 us; the launch traced here: 1190 us
  waiting for transfers between devices  643 us (54%)
  other arithmetic  175 us (15%)
  matrix products  173 us (14%)
  local copies, waits for them, and re-layouts  135 us (11%)
  blocking collectives  44.8 us (4%)
  between operations  17.6 us (1%)
    reduce_scatter x1, waiting for transfers between devices, on_device(): lax.psum_scatter(grad_up, 'dp', scatter_dimension=0, tiled=True)  141 us
    reduce_scatter x1, waiting for transfers between devices, on_device(): lax.psum_scatter(grad_down, 'dp', scatter_dimension=0, tiled=True)  141 us
    unnamed x1, other arithmetic  113 us
    reduce_scatter x1, waiting for transfers between devices, on_device(): lax.psum_scatter(grad_query_self, 'dp', scatter_dimension=0, tiled=True)  66.6 us
    reduce_scatter x1, waiting for transfers between devices, on_device(): lax.psum_scatter(grad_value_self, 'dp', scatter_dimension=0, tiled=True)  66.5 us
    reduce_scatter x1, waiting for transfers between devices, on_device(): lax.psum_scatter(grad_key_self, 'dp', scatter_dimension=0, tiled=True)  66.1 us
    reduce_scatter x1, waiting for transfers between devices, on_device(): lax.psum_scatter(grad_out_self, 'dp', scatter_dimension=0, tiled=True)  66.1 us
    unnamed x171, local copies, waits for them, and re-layouts  63.8 us
  transfers between devices with their start and end apart: 13, of which 8 were waited for; matrix products, arithmetic and copies ran while one was open for 20% of the time, Pallas kernels for 0%

commit v1 on v0

v1 whole, which is shorter than its diff:
```python
import functools
import math

import jax
import jax.numpy as jnp
from jax import lax
from jax.experimental import pallas as pl
from jax.experimental.pallas import tpu as pltpu
from jax.sharding import PartitionSpec as P

HEADS = 8
HEAD = 80
MAIN = 64
REST = 16
ROW_LEN = 256
BLOCK = 256
SCALE = 1.0 / math.sqrt(HEAD)
LOW = jnp.bfloat16
FULL = jnp.float32
VMEM_BYTES = 56 * 1024 * 1024


def dot(left, right, left_dim, right_dim):
    return lax.dot_general(
        left, right, (((left_dim,), (right_dim,)), ((), ())), preferred_element_type=FULL
    )


def nn(left, right):
    return dot(left, right, 1, 0)


def nt(left, right):
    return dot(left, right, 1, 1)


def tn(left, right):
    return dot(left, right, 0, 0)


def norm_parts(value):
    centred = value - jnp.mean(value, axis=-1, keepdims=True)
    inverse = lax.rsqrt(jnp.mean(centred * centred, axis=-1, keepdims=True) + 1e-05)
    return (centred * inverse, inverse)


def norm_forward(value, gain):
    return (norm_parts(value)[0] * gain).astype(LOW)


def norm_backward(grad, value, gain):
    normed, inverse = norm_parts(value)
    scaled = grad * gain
    inner = (
        scaled
        - jnp.mean(scaled, axis=-1, keepdims=True)
        - normed * jnp.mean(scaled * normed, axis=-1, keepdims=True)
    )
    return inner * inverse


def source_column(position):
    rest = position - HEADS * MAIN
    return jnp.where(
        rest < 0,
        HEAD * (position // MAIN) + position % MAIN,
        HEAD * (rest // REST) + MAIN + rest % REST,
    )


def order_matrix(width, transposed):
    rows = lax.broadcasted_iota(jnp.int32, (width, width), 0)
    columns = lax.broadcasted_iota(jnp.int32, (width, width), 1)
    if transposed:
        rows, columns = columns, rows
    return (rows == source_column(columns)).astype(FULL).astype(LOW)


def head_groups(array, head):
    pair = head // 2
    return jnp.concatenate(
        [array[:, 2 * MAIN * pair : 2 * MAIN * (pair + 1)], array[:, HEADS * MAIN :]], axis=1
    )


def head_mask(head):
    lane = lax.broadcasted_iota(jnp.int32, (1, 2 * MAIN + HEADS * REST), 1)
    rest = lane - 2 * MAIN
    owner = jnp.where(rest < 0, 2 * (head // 2) + lane // MAIN, rest // REST)
    return (owner == head).astype(FULL).astype(LOW)


def same_segment(key_seg, query_seg):
    shape = (16, key_seg.shape[1])
    number = lax.broadcasted_iota(jnp.int32, shape, 0)
    key_hot = (number == key_seg).astype(FULL).astype(LOW)
    query_hot = (number == query_seg).astype(FULL).astype(LOW)
    return tn(key_hot, query_hot)


def merge_heads(parts):
    mains = [
        parts[2 * pair][:, : 2 * MAIN] + parts[2 * pair + 1][:, : 2 * MAIN]
        for pair in range(HEADS // 2)
    ]
    rests = [part[:, 2 * MAIN :] for part in parts]
    while len(rests) > 1:
        rests = [rests[i] + rests[i + 1] for i in range(0, len(rests), 2)]
    return jnp.concatenate(mains + rests, axis=1)


def attend(queries, keys, values, bias, probs_ref):
    parts = []
    for head in range(HEADS):
        mask = head_mask(head)
        scores = nt(head_groups(keys, head), head_groups(queries, head) * mask) * SCALE + bias
        raised = jnp.exp(scores - jnp.max(scores, axis=0, keepdims=True))
        probs = (raised * (1.0 / jnp.sum(raised, axis=0, keepdims=True))).astype(LOW)
        probs_ref[0, head] = probs
        parts.append(tn(probs, head_groups(values, head) * mask))
    return merge_heads(parts).astype(LOW)


def attend_back(grad, queries, keys, values, probs_ref):
    query_parts, key_parts, value_parts = [], [], []
    for head in range(HEADS):
        mask = head_mask(head)
        grad_head = head_groups(grad, head) * mask
        probs = probs_ref[0, head]
        wide = probs.astype(FULL)
        prob_grad = nt(head_groups(values, head), grad_head)
        delta = jnp.sum(prob_grad * wide, axis=0, keepdims=True)
        score_grad = (wide * (prob_grad - delta)).astype(LOW)
        value_parts.append(nn(probs, grad_head))
        key_parts.append(nn(score_grad, head_groups(queries, head) * mask))
        query_parts.append(tn(score_grad, head_groups(keys, head) * mask))
    return (
        (merge_heads(query_parts) * SCALE).astype(LOW),
        (merge_heads(key_parts) * SCALE).astype(LOW),
        merge_heads(value_parts).astype(LOW),
    )


def order_kernel(*refs):
    count = len(refs) // 2
    order = order_matrix(refs[0].shape[0], False)
    for source, target in zip(refs[: count - 2], refs[count:-2]):
        target[...] = nn(source[...], order).astype(LOW)
    for source, target in zip(refs[count - 2 : count], refs[-2:]):
        for head in range(HEADS):
            base = HEAD * head
            target[MAIN * head : MAIN * (head + 1)] = source[base : base + MAIN]
            rest = HEADS * MAIN + REST * head
            target[rest : rest + REST] = source[base + MAIN : base + HEAD]


def self_forward_kernel(
    x_ref, seg_ref, gain_ref, next_gain_ref, wq_ref, wk_ref, wv_ref, wo_ref, next_wq_ref,
    normed_ref, q_ref, k_ref, v_ref, probs_ref, attn_ref, after_ref, next_normed_ref, next_q_ref,
):
    value = x_ref[...].astype(FULL)
    normed = norm_forward(value, gain_ref[...])
    normed_ref[...] = normed
    queries = nn(normed, wq_ref[...]).astype(LOW)
    keys = nn(normed, wk_ref[...]).astype(LOW)
    values = nn(normed, wv_ref[...]).astype(LOW)
    q_ref[...], k_ref[...], v_ref[...] = queries, keys, values
    seg = seg_ref[0]
    key_at = lax.broadcasted_iota(jnp.int32, (ROW_LEN, ROW_LEN), 0)
    query_at = lax.broadcasted_iota(jnp.int32, (ROW_LEN, ROW_LEN), 1)
    allowed = (same_segment(seg, seg) > 0.5) & (key_at <= query_at)
    attn = attend(queries, keys, values, jnp.where(allowed, 0.0, -1e9), probs_ref)
    attn_ref[...] = attn
    after = value + nn(attn, wo_ref[...])
    after_ref[...] = after
    next_normed = norm_forward(after, next_gain_ref[...])
    next_normed_ref[...] = next_normed
    next_q_ref[...] = nn(next_normed, next_wq_ref[...]).astype(LOW)


def cross_forward_kernel(
    near_ref, far_ref, q_ref, after_ref, seg_target_ref, seg_source_ref, gain_ref, wk_ref, wv_ref, wo_ref,
    memory_ref, k_ref, v_ref, probs_ref, attn_ref, next_after_ref, next_normed_ref,
):
    memory = (near_ref[...].astype(FULL) + far_ref[...].astype(FULL)).astype(LOW)
    memory_ref[...] = memory
    keys = nn(memory, wk_ref[...]).astype(LOW)
    values = nn(memory, wv_ref[...]).astype(LOW)
    k_ref[...], v_ref[...] = keys, values
    allowed = same_segment(seg_source_ref[0], seg_target_ref[0]) > 0.5
    attn = attend(q_ref[...], keys, values, jnp.where(allowed, 0.0, -1e9), probs_ref)
    attn_ref[...] = attn
    after = after_ref[...] + nn(attn, wo_ref[...])
    next_after_ref[...] = after
    next_normed_ref[...] = norm_forward(after, gain_ref[...])


def put_chunk(place_ref, keep_ref, send_ref, quarter, chunk, columns, piece):
    x_at = lax.bitwise_xor(quarter // 2, lax.shift_right_logical(place_ref[0], 1))
    core = lax.bitwise_and(place_ref[0], 1)
    dp_at = lax.bitwise_xor(chunk, place_ref[1])

    @pl.when(core == quarter % 2)
    def _():
        keep_ref[x_at, dp_at, :, columns] = piece

    @pl.when(core != quarter % 2)
    def _():
        send_ref[x_at, dp_at, :, columns] = piece


def feed_kernel(
    chunks, place_ref, normed_ref, grad_ref, up_ref, down_ref, after_ref, *refs
):
    if chunks:
        out_ref, back_ref, up_keep, up_send, down_keep, down_send = refs[:6]
    else:
        out_ref, back_ref, up_all, down_all = refs[:4]
    acc_ref, normed_t, grad_t, hidden_ref, pre_ref = refs[-5:]
    step = pl.program_id(0)
    tokens, width = normed_ref.shape
    share = up_ref.shape[1]

    @pl.when(step == 0)
    def _():
        acc_ref[...] = after_ref[...]
        back_ref[...] = jnp.zeros_like(back_ref)
        for start in range(0, tokens, BLOCK):
            rows = slice(start, start + BLOCK)
            normed_t[:, rows] = normed_ref[rows, :].T
            grad_t[:, rows] = grad_ref[rows, :].T

    @pl.loop(0, tokens // BLOCK)
    def _(at):
        rows = pl.ds(pl.multiple_of(at * BLOCK, BLOCK), BLOCK)
        pre = nn(normed_ref[rows, :], up_ref[...])
        square = pre * pre
        slope = math.sqrt(2.0 / math.pi)
        bend = jnp.tanh(slope * pre * (1.0 + 0.044715 * square))
        half = 0.5 * (1.0 + bend)
        hidden = (pre * half).astype(LOW)
        rate = half + 0.5 * pre * (1.0 - bend * bend) * (slope * (1.0 + 3 * 0.044715 * square))
        pre_grad = (nt(grad_ref[rows, :], down_ref[...]) * rate).astype(LOW)
        hidden_ref[rows, :] = hidden
        pre_ref[rows, :] = pre_grad
        acc_ref[rows, :] += nn(hidden, down_ref[...])
        back_ref[rows, :] += nt(pre_grad, up_ref[...])

    for start in range(0, share, BLOCK):
        columns = slice(start, start + BLOCK)
        up_grad = nn(normed_t[...], pre_ref[:, columns]).astype(LOW)
        down_grad = nn(grad_t[...], hidden_ref[:, columns]).astype(LOW).T
        if not chunks:
            up_all[:, columns] = up_grad
            down_all[columns, :] = down_grad
            continue
        length = width // chunks
        x_at = lax.bitwise_xor(step // 2, lax.shift_right_logical(place_ref[0], 1))
        core = lax.bitwise_and(place_ref[0], 1)
        for chunk in range(chunks):
            piece = up_grad[length * chunk : length * (chunk + 1)]
            dp_at = lax.bitwise_xor(chunk, place_ref[1])

            @pl.when(core == step % 2)
            def _():
                up_keep[x_at, dp_at, :, columns] = piece

            @pl.when(core != step % 2)
            def _():
                up_send[x_at, dp_at, :, columns] = piece

        part = share // 8
        for row in range(start, start + BLOCK, 32):
            chunk = 2 * step + row // (share // 2)
            inside = row % (share // 2)
            quarter, offset = inside // part, inside % part
            x_at = lax.bitwise_xor(quarter // 2, lax.shift_right_logical(place_ref[0], 1))
            dp_at = lax.bitwise_xor(chunk, place_ref[1])
            piece = down_grad[row - start : row - start + 32]
            target = slice(offset, offset + 32)

            @pl.when(core == quarter % 2)
            def _():
                down_keep[x_at, dp_at, target, :] = piece

            @pl.when(core != quarter % 2)
            def _():
                down_send[x_at, dp_at, target, :] = piece

    @pl.when(step == pl.num_programs(0) - 1)
    def _():
        out_ref[...] = acc_ref[...].astype(LOW)


def cross_backward_kernel(
    back_ref, after_cross_ref, gain_feed_ref, grad_ref, after_self_ref, gain_cross_ref,
    q_ref, k_ref, v_ref, probs_ref, wq_ref, wk_ref, wv_ref, wo_ref,
    in_ref, dq_ref, dk_ref, dv_ref, memory_ref, grad_self_ref,
):
    grad = grad_ref[...].astype(FULL) + norm_backward(
        back_ref[...], after_cross_ref[...], gain_feed_ref[...]
    )
    branch = grad.astype(LOW)
    in_ref[...] = branch
    query_grad, key_grad, value_grad = attend_back(
        nt(branch, wo_ref[...]).astype(LOW), q_ref[...], k_ref[...], v_ref[...], probs_ref
    )
    dq_ref[...], dk_ref[...], dv_ref[...] = query_grad, key_grad, value_grad
    memory_ref[...] = (nt(key_grad, wk_ref[...]) + nt(value_grad, wv_ref[...])).astype(LOW)
    grad_self_ref[...] = grad + norm_backward(
        nt(query_grad, wq_ref[...]), after_self_ref[...], gain_cross_ref[...]
    )


def self_backward_kernel(
    grad_ref, q_ref, k_ref, v_ref, probs_ref, wo_ref, in_ref, dq_ref, dk_ref, dv_ref
):
    branch = grad_ref[...].astype(LOW)
    in_ref[...] = branch
    dq_ref[...], dk_ref[...], dv_ref[...] = attend_back(
        nt(branch, wo_ref[...]).astype(LOW), q_ref[...], k_ref[...], v_ref[...], probs_ref
    )


def input_grad_kernel(dq_ref, dk_ref, dv_ref, wq_ref, wk_ref, wv_ref, x_ref, gain_ref, grad_ref, out_ref):
    inner = (
        nt(dq_ref[...], wq_ref[...]) + nt(dk_ref[...], wk_ref[...]) + nt(dv_ref[...], wv_ref[...])
    )
    back = norm_backward(inner, x_ref[...].astype(FULL), gain_ref[...])
    out_ref[...] = (grad_ref[...] + back).astype(LOW)


def weight_kernel(chunks, sources, place_ref, *refs):
    lefts = refs[: max(sources) + 1]
    rights = refs[len(lefts) : len(lefts) + 4]
    targets, left_t = refs[len(lefts) + 4 : -1], refs[-1]
    tokens, width = rights[0].shape
    ready = None
    for weight in range(4):
        if sources[weight] != ready:
            ready = sources[weight]
            for start in range(0, tokens, BLOCK):
                rows = slice(start, start + BLOCK)
                left_t[:, rows] = lefts[ready][rows, :].T
        for start in range(0, width, BLOCK):
            columns = slice(start, min(start + BLOCK, width))
            grad = nn(left_t[...], rights[weight][:, columns]).astype(LOW)
            if not chunks:
                targets[0][weight, :, columns] = grad
                continue
            length = width // chunks
            for chunk in range(chunks):
                piece = grad[length * chunk : length * (chunk + 1)]
                if weight == 3:
                    rest = HEADS * MAIN + REST * chunk
                    piece = jnp.concatenate(
                        [grad[MAIN * chunk : MAIN * (chunk + 1)], grad[rest : rest + REST]], axis=0
                    )
                put_chunk(place_ref, *targets, weight, chunk, columns, piece)


def encoder_grad_kernel(place_ref, hits_ref, *refs):
    out_ref = refs[-1]
    step = pl.program_id(0)
    rows = pl.num_programs(0) // 4
    for turn in range(4):

        @pl.when(step // rows == turn)
        def _():
            owner = lax.bitwise_xor(place_ref[0], turn)
            weight = 0.5 * hits_ref[owner * rows + step % rows]
            out_ref[0] = weight * refs[turn][...].astype(FULL)


def final_kernel(place_ref, *refs):
    sources, weights, gains, targets = refs[:16], refs[16:21], refs[21:24], refs[24:-2]
    cross_ref, self_ref = refs[-2:]
    up_out, down_out = targets[8:10]
    part = down_out.shape[0] // 4
    share = up_out.shape[1] // 4
    for turn in range(4):
        up, down, cross, own = sources[4 * turn : 4 * (turn + 1)]
        owner = lax.bitwise_xor(place_ref[0], turn)
        up_out[:, pl.ds(pl.multiple_of(owner * share, share), share)] = up[...].astype(FULL)
        down_out[pl.ds(pl.multiple_of(owner * part, part), part), :] = down[...].astype(FULL)
        cross_ref[owner] = cross[...]
        self_ref[owner] = own[...]
    order = order_matrix(cross_ref.shape[2], True)
    for at in range(3):
        targets[at][...] = nn(self_ref[at], order)
        targets[4 + at][...] = nn(cross_ref[at], order)
    targets[3][...] = self_ref[3].astype(FULL)
    targets[7][...] = cross_ref[3].astype(FULL)

    def gain_grad(pairs, gain_ref, target):
        total = sum(
            jnp.sum(weight.astype(FULL) * grad.astype(FULL), axis=1, keepdims=True)
            for weight, grad in pairs
        )
        turned = jnp.broadcast_to(total, (total.shape[0], 128)).T
        target[0] = turned[:1] / gain_ref[0]

    gain_grad([(weights[at][...], self_ref[at]) for at in range(3)], gains[0], targets[10])
    gain_grad([(weights[3][...], cross_ref[0])], gains[1], targets[11])
    gain_grad([(weights[4][...], up_out[...])], gains[2], targets[12])


def whole(array):
    return pl.BlockSpec(array.shape, lambda *at: (0,) * array.ndim)


def by_row(array):
    if array.ndim == 2:
        return pl.BlockSpec((ROW_LEN, array.shape[1]), lambda at, *_: (at, 0))
    return pl.BlockSpec(
        (1,) + array.shape[1:], lambda at, *_: (at,) + (0,) * (array.ndim - 1)
    )


def run(body, name, grid, ins, in_specs, outs, out_specs, flops, scratch=(), prefetch=()):
    moved = sum(array.size * array.dtype.itemsize for array in list(ins) + list(outs))
    return pl.pallas_call(
        body,
        name=name,
        out_shape=outs,
        grid_spec=pltpu.PrefetchScalarGridSpec(
            num_scalar_prefetch=len(prefetch),
            grid=grid,
            in_specs=in_specs,
            out_specs=out_specs,
            scratch_shapes=scratch,
        ),
        compiler_params=pltpu.CompilerParams(vmem_limit_bytes=VMEM_BYTES),
        cost_estimate=pl.CostEstimate(
            flops=int(flops), bytes_accessed=int(moved), transcendentals=0
        ),
    )(*prefetch, *ins)


def shape_of(shape, dtype=LOW):
    return jax.ShapeDtypeStruct(tuple(shape), dtype)


def row_call(body, name, rowed, fixed, outs, flops, order):
    ins, specs = [], []
    rowed, fixed = list(rowed), list(fixed)
    for kind in order:
        array = rowed.pop(0) if kind == "r" else fixed.pop(0)
        ins.append(array)
        specs.append(by_row(array) if kind == "r" else whole(array))
    tokens = outs[0].shape[0]
    return run(
        body, name, (tokens // ROW_LEN,), ins, specs, outs, [by_row(out) for out in outs], flops
    )


def permuted(value, axes, sizes, flip):
    count = math.prod(sizes)
    return lax.ppermute(value, axes, [(at, at ^ flip) for at in range(count)])


def added(parts):
    total = parts[0].astype(FULL)
    for part in parts[1:]:
        total = total + part.astype(FULL)
    return total.astype(LOW)


def on_device(
    layer_size,
    dp_size,
    inputs,
    encoder_out,
    query_self,
    key_self,
    value_self,
    out_self,
    query_cross,
    key_cross,
    value_cross,
    out_cross,
    feed_up,
    feed_down,
    gain_self,
    gain_cross,
    gain_feed,
    seg_target,
    seg_source,
    subnet_of_row,
    chosen_layers,
    out_grad,
):
    tokens, width = inputs.shape
    rows = tokens // ROW_LEN
    layer_at = lax.axis_index("layer")
    dp_at = lax.axis_index("dp")
    place = jnp.stack([layer_at, dp_at]).astype(jnp.int32)
    axes, sizes = ("dp", "layer"), (dp_size, layer_size)

    def across(value, layer_flip, dp_flip=0):
        return permuted(value, axes, sizes, dp_flip * layer_size + layer_flip)

    picked = jnp.sum(
        (chosen_layers[:, :, None] == jnp.arange(layer_size)[None, None, :]).astype(FULL), axis=1
    )
    row_pick = (subnet_of_row[:, None] == jnp.arange(chosen_layers.shape[0])[None, :]).astype(FULL)
    block_hits = jnp.sum(row_pick[:, :, None] * picked[None], axis=1)
    own_layer = encoder_out.reshape(layer_size, rows, ROW_LEN, width)

    def own_block(flip):
        return lax.dynamic_index_in_dim(own_layer, layer_at ^ flip, 0, keepdims=False)

    def hits_of(flip, layer_flip):
        hits = lax.dynamic_slice_in_dim(block_hits, (layer_at ^ flip) * rows, rows, 0)
        hits = lax.dynamic_slice_in_dim(hits, layer_at ^ layer_flip, 1, 1)
        return 0.5 * hits[:, :, None]

    def chip_sum(flip, arrived):
        total = hits_of(flip, 0) * own_block(flip).astype(FULL)
        total = total + hits_of(flip, 1) * arrived.astype(FULL)
        return total.astype(LOW).reshape(tokens, width)

    far_half = across(own_block(3), 1)
    near_half = across(own_block(1), 1)
    far_memory = across(chip_sum(2, far_half), 2)
    near_memory = chip_sum(0, near_half)

    weights = [query_self, key_self, value_self, query_cross, key_cross, value_cross, out_self, out_cross]
    ordered = run(
        order_kernel,
        "order_weights",
        (1,),
        weights,
        [whole(array) for array in weights],
        [shape_of(array.shape) for array in weights],
        [whole(array) for array in weights],
        12 * width**3,
    )
    wq_self, wk_self, wv_self, wq_cross, wk_cross, wv_cross, wo_self, wo_cross = ordered
    target = seg_target.reshape(rows, 1, ROW_LEN)
    source = seg_source.reshape(rows, 1, ROW_LEN)
    g_self, g_cross, g_feed = (gain.reshape(1, width) for gain in (gain_self, gain_cross, gain_feed))
    flat = shape_of((tokens, width))
    wide = shape_of((tokens, width), FULL)
    probs = shape_of((rows, HEADS, ROW_LEN, ROW_LEN))
    dense_flops = 2 * tokens * width * width
    head_flops = 2 * tokens * ROW_LEN * ROW_LEN * HEADS

    normed_self, q_self, k_self, v_self, probs_self, attn_self, after_self, normed_cross, q_cross = row_call(
        self_forward_kernel,
        "self_forward",
        (inputs, target),
        (g_self, g_cross, wq_self, wk_self, wv_self, wo_self, wq_cross),
        [flat, flat, flat, flat, probs, flat, wide, flat, flat],
        5 * dense_flops + 2 * head_flops,
        "rrfffffff",
    )
    memory, k_cross, v_cross, probs_cross, attn_cross, after_cross, normed_feed = row_call(
        cross_forward_kernel,
        "cross_forward",
        (near_memory, far_memory, q_cross, after_self, target, source),
        (g_feed, wk_cross, wv_cross, wo_cross),
        [flat, flat, flat, probs, flat, wide, flat],
        3 * dense_flops + 2 * head_flops,
        "rrrrrrffff",
    )

    chunks = dp_size if dp_size == HEADS and layer_size == 4 else 0
    hidden = feed_up.shape[1]
    share = hidden // 4
    if chunks:
        up_shape = shape_of((2, chunks, width // chunks, share))
        down_shape = shape_of((2, chunks, share // 8, width))
        feed_outs = [up_shape, up_shape, down_shape, down_shape]
        feed_specs = [whole(out) for out in feed_outs]
        weight_outs = [shape_of((2, chunks, width // chunks, width))] * 2
    else:
        feed_outs = [shape_of(feed_up.shape), shape_of(feed_down.shape)]
        feed_specs = [
            pl.BlockSpec((width, share), lambda at, *_: (0, at)),
            pl.BlockSpec((share, width), lambda at, *_: (at, 0)),
        ]
        weight_outs = [shape_of((4, width, width))]
    layer_out, back_feed, *feed_grads = run(
        functools.partial(feed_kernel, chunks),
        "feed",
        (4,),
        [normed_feed, out_grad, feed_up, feed_down, after_cross],
        [
            whole(normed_feed),
            whole(out_grad),
            pl.BlockSpec((width, share), lambda at, *_: (0, at)),
            pl.BlockSpec((share, width), lambda at, *_: (at, 0)),
            whole(after_cross),
        ],
        [flat, wide] + feed_outs,
        [whole(flat), whole(wide)] + feed_specs,
        12 * tokens * width * hidden,
        scratch=[
            pltpu.VMEM((tokens, width), FULL),
            pltpu.VMEM((width, tokens), LOW),
            pltpu.VMEM((width, tokens), LOW),
            pltpu.VMEM((tokens, share), LOW),
            pltpu.VMEM((tokens, share), LOW),
        ],
        prefetch=(place,),
    )

    def weight_call(name, sources, lefts, rights):
        ins = list(lefts) + list(rights)
        return run(
            functools.partial(weight_kernel, chunks, sources),
            name,
            (1,),
            ins,
            [whole(array) for array in ins],
            weight_outs,
            [whole(out) for out in weight_outs],
            4 * dense_flops,
            scratch=[pltpu.VMEM((width, tokens), LOW)],
            prefetch=(place,),
        )

    cross_in, dq_cross, dk_cross, dv_cross, memory_grad, grad_after_self = row_call(
        cross_backward_kernel,
        "cross_backward",
        (back_feed, after_cross, out_grad, after_self, q_cross, k_cross, v_cross, probs_cross),
        (g_feed, g_cross, wq_cross, wk_cross, wv_cross, wo_cross),
        [flat, flat, flat, flat, flat, wide],
        4 * dense_flops + 4 * head_flops,
        "rrfrrfrrrrffff",
    )
    cross_grads = weight_call(
        "cross_weights",
        (0, 1, 1, 2),
        (normed_cross, memory, attn_cross),
        (dq_cross, dk_cross, dv_cross, cross_in),
    )
    self_in, dq_self, dk_self, dv_self = row_call(
        self_backward_kernel,
        "self_backward",
        (grad_after_self, q_self, k_self, v_self, probs_self),
        (wo_self,),
        [flat, flat, flat, flat],
        dense_flops + 4 * head_flops,
        "rrrrrf",
    )
    self_grads = weight_call(
        "self_weights",
        (0, 0, 0, 1),
        (normed_self, attn_self),
        (dq_self, dk_self, dv_self, self_in),
    )
    (input_grad,) = row_call(
        input_grad_kernel,
        "input_grad",
        (dq_self, dk_self, dv_self, inputs, grad_after_self),
        (wq_self, wk_self, wv_self, g_self),
        [flat],
        3 * dense_flops,
        "rrrfffrfr",
    )

    from_core = across(memory_grad, 1)
    from_chip = across(memory_grad, 2)
    from_both = across(from_chip, 1)
    own_hits = lax.dynamic_slice_in_dim(block_hits, layer_at, 1, 1)[:, 0]
    arrived = [memory_grad, from_core, from_chip, from_both]

    def arrived_spec(turn):
        return pl.BlockSpec(
            (ROW_LEN, width), lambda at, *_: (jnp.clip(at - turn * rows, 0, rows - 1), 0)
        )

    encoder_shape = shape_of(encoder_out.shape, FULL)
    (encoder_grad,) = run(
        encoder_grad_kernel,
        "encoder_grad",
        (4 * rows,),
        arrived,
        [arrived_spec(turn) for turn in range(4)],
        [encoder_shape],
        [
            pl.BlockSpec(
                (1, ROW_LEN, width),
                lambda at, place, hits: (0, (place[0] ^ (at // rows)) * rows + at % rows, 0),
            )
        ],
        encoder_out.size,
        prefetch=(place, own_hits),
    )

    if chunks:

        def scatter(keep, send):
            parts = [part.reshape((2, 4, 2) + part.shape[2:]) for part in (keep, across(send, 1))]
            x_send = added([part[1, :, 0] for part in parts])
            y_send = added([part[0, :, 1] for part in parts])
            both_send = added([part[1, :, 1] for part in parts])
            parts = [part[0, :, 0] for part in parts]
            parts += [across(both_send, 2, 1), across(x_send, 2), across(y_send, 0, 1)]
            sends = [added([part[flip] for part in parts]) for flip in (1, 2, 3)]
            arrived = [across(sends[flip - 1], 0, 2 * flip) for flip in (1, 2, 3)]
            return added([part[0] for part in parts] + arrived)

        pieces = [
            scatter(feed_grads[0], feed_grads[1]),
            scatter(feed_grads[2], feed_grads[3]),
            scatter(*cross_grads),
            scatter(*self_grads),
        ]
        gathered = pieces + [across(piece, flip) for flip in (1, 2, 3) for piece in pieces]
        length = width // chunks
        square = shape_of((length, width), FULL)
        outs = [square] * 8 + [
            shape_of((length, hidden), FULL),
            shape_of((hidden // chunks, width), FULL),
        ]
        outs += [shape_of((1, 1, length), FULL)] * 3
        chunk_weights = [wq_self, wk_self, wv_self, wq_cross, feed_up]
        gains = [gain.reshape(chunks, 1, length) for gain in (gain_self, gain_cross, gain_feed)]
        finals = run(
            final_kernel,
            "final",
            (1,),
            gathered + chunk_weights + gains,
            [whole(array) for array in gathered]
            + [
                pl.BlockSpec((length, array.shape[1]), lambda at, place: (place[1], 0))
                for array in chunk_weights
            ]
            + [pl.BlockSpec((1, 1, length), lambda at, place: (place[1], 0, 0))] * 3,
            outs,
            [whole(out) for out in outs],
            12 * length * width * width,
            scratch=[pltpu.VMEM((4, length, width), LOW)] * 2,
            prefetch=(place,),
        )
        weight_grads = list(finals[:10])
        gain_grads = [value.reshape(length) for value in finals[10:]]
    else:
        back_order = order_matrix(width, True)

        def total(grad):
            part = lax.psum_scatter(grad.astype(FULL), "dp", scatter_dimension=0, tiled=True)
            return lax.psum(part.astype(LOW), "layer").astype(FULL)

        def natural(grads):
            back = [nn(grads[0][at], back_order).astype(LOW) for at in range(3)]
            return [total(grad) for grad in back + [nn(back_order.T, grads[0][3]).astype(LOW)]]

        grads_self, grads_cross = natural(self_grads), natural(cross_grads)
        weight_grads = grads_self + grads_cross + [total(grad) for grad in feed_grads]
        length = width // dp_size

        def my_rows(array):
            return lax.dynamic_slice_in_dim(array, dp_at * length, length, 0).astype(FULL)

        def gain_total(pairs, gain):
            sums = sum(jnp.sum(my_rows(weight) * grad, axis=1) for weight, grad in pairs)
            return sums / my_rows(gain)

        gain_grads = [
            gain_total(zip((query_self, key_self, value_self), grads_self), gain_self),
            gain_total([(query_cross, grads_cross[0])], gain_cross),
            gain_total([(feed_up, weight_grads[8])], gain_feed),
        ]
    return (layer_out, input_grad, encoder_grad, *weight_grads, *gain_grads)


def solution(mesh):
    in_specs = (
        P(("dp", "layer"), None),
        P("layer", "dp", None),
        *[P()] * 13,
        P(("dp", "layer"), None),
        P(("dp", "layer"), None),
        P("dp"),
        P(),
        P(("dp", "layer"), None),
    )
    out_specs = (
        P(("dp", "layer"), None),
        P(("dp", "layer"), None),
        P("layer", "dp", None),
        *[P("dp", None)] * 10,
        *[P("dp")] * 3,
    )
    body = functools.partial(on_device, mesh.shape["layer"], mesh.shape["dp"])
    return jax.shard_map(
        body, mesh=mesh, in_specs=in_specs, out_specs=out_specs, check_vma=False
    )
```

time: 1200 us -> 361 us (0.30)
  waiting for transfers between devices: 643 us -> 86 us
  Pallas kernels: 0 us -> 186 us
  matrix products: 173 us -> 0 us
  other arithmetic: 175 us -> 20.9 us
  local copies, waits for them, and re-layouts: 135 us -> 12.6 us
  blocking collectives: 44.8 us -> 0 us
  starting transfers between devices: 6.84 us -> 48.8 us
  between operations: 17.6 us -> 1.32 us
    reduce_scatter x10 -> x0, waiting for transfers between devices: 603 us -> none  [the longest x1 141 us: on_device(): lax.psum_scatter(grad_up, 'dp', scatter_dimension=0, tiled=True)]
    pallas_call x0 -> x11, Pallas kernels: none -> 186 us  [run(): pl.pallas_call(body, name=name, out_shape=outs, grid_spec=pltpu.PrefetchS...]
    dot_general x44 -> x0, matrix products: 173 us -> none  [the longest x10 44.9 us: dense_back(): lax.dot_general(grad, weight, (((1,), (1,)), ((), ())), preferred_element...]
    unnamed x1 -> x0, other arithmetic: 113 us -> none
    ppermute x0 -> x46, waiting for transfers between devices: none -> 86 us  [permuted(): return lax.ppermute(value, axes, [(at, at ^ flip) for at in range(count)])]
    unnamed x171 -> x70, local copies, waits for them, and re-layouts: 63.8 us -> 4.01 us
    reshape x16 -> x8, local copies, waits for them, and re-layouts: 62.8 us -> 4.95 us  [the longest x3 2.02 us: on_device(): gain.reshape(chunks, 1, length)]
    ppermute x0 -> x46, starting transfers between devices: none -> 48.8 us  [permuted(): return lax.ppermute(value, axes, [(at, at ^ flip) for at in range(count)])]
  transfers between devices with their start and end apart: 13 -> 46, of which waited for: 8 -> 19; matrix products, arithmetic and copies ran while one was open for 20% -> 6% of each run, Pallas kernels for 0% -> 18%
where the time goes in v1:
time: 361 us; the launch traced here: 356 us
  Pallas kernels  186 us (52%)
  waiting for transfers between devices  86 us (24%)
  starting transfers between devices  48.8 us (14%)
  other arithmetic  20.9 us (6%)
  local copies, waits for them, and re-layouts  12.6 us (3%)
    pallas_call x11, Pallas kernels, run(): pl.pallas_call(body, name=name, out_shape=outs, grid_spec=pltpu.PrefetchS...  186 us
    ppermute x46, waiting for transfers between devices, permuted(): return lax.ppermute(value, axes, [(at, at ^ flip) for at in range(count)])  86 us
    ppermute x46, starting transfers between devices, permuted(): return lax.ppermute(value, axes, [(at, at ^ flip) for at in range(count)])  48.8 us
    convert_element_type x12, other arithmetic, added(): return total.astype(LOW)  15.8 us
  transfers between devices with their start and end apart: 46, of which 19 were waited for; matrix products, arithmetic and copies ran while one was open for 6% of the time, Pallas kernels for 18%

profile of v1, /device:TPU:0, one launch (start us, length us, event | category | flops | bytes accessed | tf_op | source)
XLA Modules:
  0.0 355.7 jit_solution(4107206260291344248)
XLA Ops:
  0.7 3.0 dynamic-slice_bitcast_fusion
  4.5 3.8 %collective-permute-done = bf16[4,256,640]{2,1,0:T(8,128)(2,1)S(1)} collective-permute-done((bf16[4,256,640]{2,1,0:T(8,128)(2,1)}, bf16[4,256,640]{2,1,0:T(8,128)(2,1)S(1)}, u32[]{:S(2)}, u32[]{:S(2)}) %collective-permute-start) | collective-permute-done | bytes 1310752 | tf_op jit(solution)/shard_map/ppermute | solution.py:459
  8.8 4.3 %fusion.1 = (bf16[4,256,640]{2,1,0:T(8,128)(2,1)S(1)}, bf16[4,256,640]{2,1,0:T(8,128)(2,1)}) fusion(bf16[4,256,640]{2,1,0:T(8,128)(2,1)} %collective-permute-done.1, f32[4]{0:T(128)S(1)} %get-tuple-element.159, bf16[4,4,256,640]{3,2,1,0:T(8,128)(2,1)} %bitcast.333, s32[]{:T(128)S(6)} %select_n.42, f32[4]{0:T(128)S(1)} %get-tuple-element.158, ...), kind=kLoop, calls=%fused_computation.2 | loop fusion | flops 7864320 | bytes 7864392 | tf_op jit(solution)/shard_map/convert_element_type | solution.py:521
  13.1 2.9 collective-permute-start.2
  19.6 8.9 %order_weights.1 = (bf16[640,640]{1,0:T(8,128)(2,1)}, bf16[640,640]{1,0:T(8,128)(2,1)}, bf16[640,640]{1,0:T(8,128)(2,1)}, bf16[640,640]{1,0:T(8,128)(2,1)}, bf16...) custom-call(bf16[640,640]{1,0:T(8,128)(2,1)} %refs_0_.1, ...), custom_call_target="tpu_custom_call" | custom-call | flops 3145728000 | bytes 13107200 | tf_op jit(solution)/shard_map/order_weights/pallas_call | solution.py:422
  28.5 17.1 %self_forward.1 = (bf16[1024,640]{1,0:T(8,128)(2,1)}, bf16[1024,640]{1,0:T(8,128)(2,1)}, bf16[1024,640]{1,0:T(8,128)(2,1)}, bf16[1024,640]{1,0:T(8,128)(2,1)}, b...) custom-call(bf16[1024,640]{1,0:T(8,128)(2,1)} %x_ref.3, ...), custom_call_target="tpu_custom_call" | custom-call | flops 6341787648 | bytes 21406720 | tf_op jit(solution)/shard_map/self_forward/pallas_call | solution.py:422
  45.7 1.0 copy-done.34
  46.7 13.8 %cross_forward.1 = (bf16[1024,640]{1,0:T(8,128)(2,1)}, bf16[1024,640]{1,0:T(8,128)(2,1)}, bf16[1024,640]{1,0:T(8,128)(2,1)}, bf16[4,8,256,256]{3,2,1,0:T(8,128)(...) custom-call(bf16[1024,640]{1,0:T(8,128)(2,1)} %bitcast.355, ...), custom_call_target="tpu_custom_call" | custom-call | flops 4664066048 | bytes 22391296 | tf_op jit(solution)/shard_map/cross_forward/pallas_call | solution.py:422
  60.6 47.3 %feed.1 = (bf16[1024,640]{1,0:T(8,128)(2,1)}, f32[1024,640]{1,0:T(8,128)}, bf16[2,8,80,768]{3,2,1,0:T(8,128)(2,1)}, bf16[2,8,80,768]{3,2,1,0:T(8,128)(2,1)}, bf1...) custom-call(s32[2]{0:T(128)} %pad_add_fusion.place_ref, bf16[1024,640]{1,0:T(8,128)(2,1)} %get-tuple-element.83.normed_ref, ...), custom_call_target="tpu_custom_call" | custom-call | flops 24159191040 | bytes 24903680 | tf_op jit(solution)/shard_map/feed/pallas_call | solution.py:422
  107.9 22.2 %cross_backward.1 = (bf16[1024,640]{1,0:T(8,128)(2,1)}, bf16[1024,640]{1,0:T(8,128)(2,1)}, bf16[1024,640]{1,0:T(8,128)(2,1)}, bf16[1024,640]{1,0:T(8,128)(2,1)},...) custom-call(f32[1024,640]{1,0:T(8,128)} %get-tuple-element.86.back_ref, ...), custom_call_target="tpu_custom_call" | custom-call | flops 7650410496 | bytes 29758464 | tf_op jit(solution)/shard_map/cross_backward/pallas_call | solution.py:422
  130.1 14.9 %self_backward.1 = (bf16[1024,640]{1,0:T(8,128)(2,1)}, bf16[1024,640]{1,0:T(8,128)(2,1)}, bf16[1024,640]{1,0:T(8,128)(2,1)}, bf16[1024,640]{1,0:T(8,128)(2,1)}) custom-call(f32[1024,640]{1,0:T(8,128)} %get-tuple-element.90.grad_ref, bf16[1024,640]{1,0:T(8,128)(2,1)} %get-tuple-element.91.q_ref, bf16[1024,640]{1,0:T(8,128)(2,1)} %get-tuple-element.92.k_ref, ...), custom_call_target="tpu_custom_call" | custom-call | flops 5133828096 | bytes 16809984 | tf_op jit(solution)/shard_map/self_backward/pallas_call | solution.py:422
  145.0 17.4 %self_weights.1 = (bf16[2,8,80,640]{3,2,1,0:T(8,128)(2,1)}, bf16[2,8,80,640]{3,2,1,0:T(8,128)(2,1)}) custom-call(s32[2]{0:T(128)} %pad_add_fusion.place_ref, bf16[1024,640]{1,0:T(8,128)(2,1)} %get-tuple-element.112.refs_0_, bf16[1024,640]{1,0:T(8,128)(2,1)} %get-tuple-element.113.refs_1_, bf16[1024,640]{1,0:T(8,128)(2,1)} %get-tuple-element.95.dq_ref.refs_2_, ...), custom_call_target="tpu_custom_call" | custom-call | flops 3355443200 | bytes 11141120 | tf_op jit(solution)/shard_map/self_weights/pallas_call | solution.py:422
  162.9 17.6 %cross_weights.1 = (bf16[2,8,80,640]{3,2,1,0:T(8,128)(2,1)}, bf16[2,8,80,640]{3,2,1,0:T(8,128)(2,1)}) custom-call(s32[2]{0:T(128)} %pad_add_fusion.place_ref, bf16[1024,640]{1,0:T(8,128)(2,1)} %get-tuple-element.103.refs_0_, bf16[1024,640]{1,0:T(8,128)(2,1)} %get-tuple-element.104.refs_1_, bf16[1024,640]{1,0:T(8,128)(2,1)} %get-tuple-element.105.refs_2_, ...), custom_call_target="tpu_custom_call" | custom-call | flops 3355443200 | bytes 12451840 | tf_op jit(solution)/shard_map/cross_weights/pallas_call | solution.py:422
  181.1 1.1 fusion.13
  182.5 2.2 collective-permute-start.28
  185.5 1.2 collective-permute-done.20
  186.6 1.2 collective-permute-start.4
  187.9 1.2 fusion.10
  189.5 6.2 %collective-permute-done.28 = bf16[4,80,640]{2,1,0:T(8,128)(2,1)S(1)} collective-permute-done((bf16[4,80,640]{2,1,0:T(8,128)(2,1)S(1)}, bf16[4,80,640]{2,1,0:T(8,128)(2,1)S(1)}, u32[]{:S(2)}, u32[]{:S(2)}) %collective-permute-start.28) | collective-permute-done | bytes 409632 | tf_op jit(solution)/shard_map/ppermute | solution.py:459
  196.5 1.5 collective-permute-start.30
  198.0 6.7 %collective-permute-done.29 = bf16[4,80,640]{2,1,0:T(8,128)(2,1)} collective-permute-done((bf16[4,80,640]{2,1,0:T(8,128)(2,1)S(1)}, bf16[4,80,640]{2,1,0:T(8,128)(2,1)}, u32[]{:S(2)}, u32[]{:S(2)}) %collective-permute-start.29) | collective-permute-done | bytes 409632 | tf_op jit(solution)/shard_map/ppermute | solution.py:459
  204.7 1.2 collective-permute-start.21
  209.2 32.3 %collective-permute-done.21 = bf16[4,80,640]{2,1,0:T(8,128)(2,1)} collective-permute-done((bf16[4,80,640]{2,1,0:T(8,128)(2,1)}, bf16[4,80,640]{2,1,0:T(8,128)(2,1)}, u32[]{:S(2)}, u32[]{:S(2)}) %collective-permute-start.21) | collective-permute-done | bytes 409632 | tf_op jit(solution)/shard_map/ppermute | solution.py:459
  241.5 1.5 collective-permute-start.23
  243.0 1.7 fusion.7
  244.8 1.7 fusion.32
  246.4 2.8 collective-permute-done.22
  249.2 1.6 collective-permute-start.31
  251.2 2.6 collective-permute-start.32
  253.8 1.5 fusion.39
  255.3 2.2 collective-permute-start.14
  258.4 1.3 collective-permute-start.33
  260.0 2.7 collective-permute-start.25
  262.8 1.7 fusion.4
  265.0 1.6 collective-permute-done.24
  266.6 3.7 %collective-permute-start.26 = (bf16[80,640]{1,0:T(8,128)(2,1)S(1)}, bf16[80,640]{1,0:T(8,128)(2,1)S(1)}, u32[]{:S(2)}, u32[]{:S(2)}) collective-permute-start(bf16[80,640]{1,0:T(8,128)(2,1)S(1)} %get-tuple-element.144), channel_id=1, source_target_pairs={{0,24},{1,25},{2,26},{3,27},{4,28},{5,29},{6,30},{7,31},{8,16},{9,... | collective-permute-start | bytes 307208 | tf_op jit(solution)/shard_map/ppermute | solution.py:459
  270.3 1.2 fusion.36.refs_3_
  271.5 1.7 collective-permute-done.26
  273.1 3.2 collective-permute-start.7
  277.2 2.4 collective-permute-done.15
  279.6 1.9 collective-permute-start.9
  281.5 1.1 fusion.43.refs_2_
  282.6 8.6 %collective-permute-done.16 = bf16[4,96,640]{2,1,0:T(8,128)(2,1)S(1)} collective-permute-done((bf16[4,96,640]{2,1,0:T(8,128)(2,1)S(1)}, bf16[4,96,640]{2,1,0:T(8,128)(2,1)S(1)}, u32[]{:S(2)}, u32[]{:S(2)}) %collective-permute-start.16) | collective-permute-done | bytes 491552 | tf_op jit(solution)/shard_map/ppermute | solution.py:459
  291.3 1.3 fusion.18
  292.6 1.3 collective-permute-start.41
  293.9 1.5 collective-permute-start.17
  295.4 4.0 %collective-permute-done.8 = bf16[4,80,768]{2,1,0:T(8,128)(2,1)S(1)} collective-permute-done((bf16[4,80,768]{2,1,0:T(8,128)(2,1)S(1)}, bf16[4,80,768]{2,1,0:T(8,128)(2,1)S(1)}, u32[]{:S(2)}, u32[]{:S(2)}) %collective-permute-start.8) | collective-permute-done | bytes 491552 | tf_op jit(solution)/shard_map/ppermute | solution.py:459
  299.3 1.2 collective-permute-start.18
  300.9 2.3 collective-permute-start.19
  303.1 1.3 fusion.25
  304.5 0.8 collective-permute-start.10
  305.3 4.4 %collective-permute-done.18 = bf16[96,640]{1,0:T(8,128)(2,1)S(1)} collective-permute-done((bf16[96,640]{1,0:T(8,128)(2,1)S(1)}, bf16[96,640]{1,0:T(8,128)(2,1)S(1)}, u32[]{:S(2)}, u32[]{:S(2)}) %collective-permute-start.18) | collective-permute-done | bytes 122912 | tf_op jit(solution)/shard_map/ppermute | solution.py:459
  310.5 1.0 fusion.22.refs_1_
  312.2 1.2 collective-permute-start.40
  313.4 6.9 %collective-permute-done.11 = bf16[80,768]{1,0:T(8,128)(2,1)S(1)} collective-permute-done((bf16[80,768]{1,0:T(8,128)(2,1)S(1)}, bf16[80,768]{1,0:T(8,128)(2,1)S(1)}, u32[]{:S(2)}, u32[]{:S(2)}) %collective-permute-start.11) | collective-permute-done | bytes 122912 | tf_op jit(solution)/shard_map/ppermute | solution.py:459
  320.3 1.3 collective-permute-start.35
  321.6 1.0 fusion.29.refs_0_
  322.7 0.9 collective-permute-start.39
  324.1 1.1 collective-permute-done.44.refs_14_
  325.3 0.9 collective-permute-start.38
  326.2 1.0 collective-permute-start.42
  327.2 8.8 %input_grad.1 = bf16[1024,640]{1,0:T(8,128)(2,1)} custom-call(bf16[1024,640]{1,0:T(8,128)(2,1)} %get-tuple-element.95.dq_ref.refs_2_, bf16[1024,640]{1,0:T(8,128)(2,1)} %get-tuple-element.96.dk_ref.refs_3_, bf16[1024,640]{1,0:T(8,128)(2,1)} %get-tuple-element.97.dv_ref.refs_4_, bf16[640,640]{1,0:T(8,128)(2,1)} %get-tuple-element.73.wq_ref.refs_16_, ...), custom_call_target="tpu_custom_call" | custom-call | flops 2516582400 | bytes 11635200 | tf_op jit(solution)/shard_map/input_grad/pallas_call | solution.py:422
  336.0 12.7 %encoder_grad.1 = f32[1,4096,640]{2,1,0:T(8,128)} custom-call(s32[2]{0:T(128)} %pad_add_fusion.place_ref, f32[16]{0:T(128)} %fusion.45.hits_ref, bf16[1024,640]{1,0:T(8,128)(2,1)} %get-tuple-element.98.refs_0_, bf16[1024,640]{1,0:T(8,128)(2,1)} %collective-permute-done.3.refs_1_, bf16[1024,640]{1,0:T(8,128)(2,1)} %collective-permute-done.4.refs_2_, ...), custom_call_target="tpu_custom_call" | custom-call | flops 2621440 | bytes 15728640 | tf_op jit(solution)/shard_map/encoder_grad/pallas_call | solution.py:422
  350.2 5.2 %final.1 = (f32[80,640]{1,0:T(8,128)}, f32[80,640]{1,0:T(8,128)}, f32[80,640]{1,0:T(8,128)}, f32[80,640]{1,0:T(8,128)}, f32[80,640]{1,0:T(8,128)}, /*index=5*/f3...) custom-call(s32[2]{0:T(128)} %pad_add_fusion.place_ref, ...), custom_call_target="tpu_custom_call" | custom-call | flops 393216000 | bytes 12624320 | tf_op jit(solution)/shard_map/final/pallas_call | solution.py:422
  (138 shorter events, 18.2 us)
Async XLA Ops:
  3.7 4.6 %collective-permute-start = (bf16[4,256,640]{2,1,0:T(8,128)(2,1)}, bf16[4,256,640]{2,1,0:T(8,128)(2,1)S(1)}, u32[]{:S(2)}, u32[]{:S(2)}) collective-permute-start(bf16[4,256,640]{2,1,0:T(8,128)(2,1)} %get-tuple-element.139), channel_id=1, source_target_pairs={{0,1},{1,0},{2,3},{3,2},{4,5},{5,4},{6,7},{7,6},{8,9},{9,8},{10,11... | collective-permute-start | bytes 3932168 | tf_op jit(solution)/shard_map/ppermute | solution.py:459
  4.2 4.7 %collective-permute-start.1 = (bf16[4,256,640]{2,1,0:T(8,128)(2,1)S(1)}, bf16[4,256,640]{2,1,0:T(8,128)(2,1)}, u32[]{:S(2)}, u32[]{:S(2)}) collective-permute-start(bf16[4,256,640]{2,1,0:T(8,128)(2,1)S(1)} %get-tuple-element.138), channel_id=1, source_target_pairs={{0,1},{1,0},{2,3},{3,2},{4,5},{5,4},{6,7},{7,6},{8,9},{9,8},{10,11... | collective-permute-start | bytes 3932168 | tf_op jit(solution)/shard_map/ppermute | solution.py:459
  8.8 8.4 %copy-start.28 = (f32[640]{0:T(1024)S(1)}, f32[640]{0:T(1024)}, u32[]{:S(2)}) copy-start(f32[640]{0:T(1024)} %param.33) | copy-start | bytes 7684
  8.8 9.0 %copy-start.29 = (f32[640]{0:T(1024)S(1)}, f32[640]{0:T(1024)}, u32[]{:S(2)}) copy-start(f32[640]{0:T(1024)} %param.34) | copy-start | bytes 7684
  8.8 9.6 %copy-start.31 = (s32[4,256]{1,0:T(4,128)S(1)}, s32[4,256]{1,0:T(4,128)}, u32[]{:S(2)}) copy-start(s32[4,256]{1,0:T(4,128)} %param.36) | copy-start | bytes 12292
  13.1 32.5 %collective-permute-start.2 = (bf16[1024,640]{1,0:T(8,128)(2,1)S(1)}, bf16[1024,640]{1,0:T(8,128)(2,1)S(1)}, u32[]{:S(2)}, u32[]{:S(2)}) collective-permute-start(bf16[1024,640]{1,0:T(8,128)(2,1)S(1)} %bitcast.356), channel_id=1, source_target_pairs={{0,2},{1,3},{2,0},{3,1},{4,6},{5,7},{6,4},{7,5},{8,10},{9,11},{10,... | collective-permute-start | bytes 3932168 | tf_op jit(solution)/shard_map/ppermute | solution.py:459
  162.4 18.7 %collective-permute-start.27 = (bf16[2,8,80,640]{3,2,1,0:T(8,128)(2,1)}, bf16[2,8,80,640]{3,2,1,0:T(8,128)(2,1)S(1)}, u32[]{:S(2)}, u32[]{:S(2)}) collective-permute-start(bf16[2,8,80,640]{3,2,1,0:T(8,128)(2,1)} %get-tuple-element.116), channel_id=1, source_target_pairs={{0,1},{1,0},{2,3},{3,2},{4,5},{5,4},{6,7},{7,6},{8,9},{9,8},{10,11... | collective-permute-start | bytes 4915208 | tf_op jit(solution)/shard_map/ppermute | solution.py:459
  162.4 25.4 %collective-permute-start.13 = (bf16[2,8,96,640]{3,2,1,0:T(8,128)(2,1)}, bf16[2,8,96,640]{3,2,1,0:T(8,128)(2,1)S(1)}, u32[]{:S(2)}, u32[]{:S(2)}) collective-permute-start(bf16[2,8,96,640]{3,2,1,0:T(8,128)(2,1)} %get-tuple-element.102), channel_id=1, source_target_pairs={{0,1},{1,0},{2,3},{3,2},{4,5},{5,4},{6,7},{7,6},{8,9},{9,8},{10,11... | collective-permute-start | bytes 5898248 | tf_op jit(solution)/shard_map/ppermute | solution.py:459
  162.9 18.2 %copy-start.5 = (bf16[2,8,80,640]{3,2,1,0:T(8,128)(2,1)S(1)}, bf16[2,8,80,640]{3,2,1,0:T(8,128)(2,1)}, u32[]{:S(2)}) copy-start(bf16[2,8,80,640]{3,2,1,0:T(8,128)(2,1)} %get-tuple-element.115) | copy-start | bytes 4915204
  180.6 6.0 %collective-permute-start.20 = (bf16[2,8,80,640]{3,2,1,0:T(8,128)(2,1)}, bf16[2,8,80,640]{3,2,1,0:T(8,128)(2,1)S(1)}, u32[]{:S(2)}, u32[]{:S(2)}) collective-permute-start(bf16[2,8,80,640]{3,2,1,0:T(8,128)(2,1)} %get-tuple-element.111), channel_id=1, source_target_pairs={{0,1},{1,0},{2,3},{3,2},{4,5},{5,4},{6,7},{7,6},{8,9},{9,8},{10,11... | collective-permute-start | bytes 4915208 | tf_op jit(solution)/shard_map/ppermute | solution.py:459
  180.6 77.8 %collective-permute-start.6 = (bf16[2,8,80,768]{3,2,1,0:T(8,128)(2,1)}, bf16[2,8,80,768]{3,2,1,0:T(8,128)(2,1)}, u32[]{:S(2)}, u32[]{:S(2)}) collective-permute-start(bf16[2,8,80,768]{3,2,1,0:T(8,128)(2,1)} %get-tuple-element.100), channel_id=1, source_target_pairs={{0,1},{1,0},{2,3},{3,2},{4,5},{5,4},{6,7},{7,6},{8,9},{9,8},{10,11... | collective-permute-start | bytes 5898248 | tf_op jit(solution)/shard_map/ppermute | solution.py:459
  182.5 13.2 %collective-permute-start.28 = (bf16[4,80,640]{2,1,0:T(8,128)(2,1)S(1)}, bf16[4,80,640]{2,1,0:T(8,128)(2,1)S(1)}, u32[]{:S(2)}, u32[]{:S(2)}) collective-permute-start(bf16[4,80,640]{2,1,0:T(8,128)(2,1)S(1)} %get-tuple-element.152), channel_id=1, source_target_pairs={{0,6},{1,7},{2,4},{3,5},{4,2},{5,3},{6,0},{7,1},{8,14},{9,15},{10,... | collective-permute-start | bytes 1228808 | tf_op jit(solution)/shard_map/ppermute | solution.py:459
  184.7 20.0 %collective-permute-start.29 = (bf16[4,80,640]{2,1,0:T(8,128)(2,1)S(1)}, bf16[4,80,640]{2,1,0:T(8,128)(2,1)}, u32[]{:S(2)}, u32[]{:S(2)}) collective-permute-start(bf16[4,80,640]{2,1,0:T(8,128)(2,1)S(1)} %get-tuple-element.154), channel_id=1, source_target_pairs={{0,2},{1,3},{2,0},{3,1},{4,6},{5,7},{6,4},{7,5},{8,10},{9,11},{10,... | collective-permute-start | bytes 1228808 | tf_op jit(solution)/shard_map/ppermute | solution.py:459
  186.6 68.7 %collective-permute-start.4 = (bf16[1024,640]{1,0:T(8,128)(2,1)S(1)}, bf16[1024,640]{1,0:T(8,128)(2,1)}, u32[]{:S(2)}, u32[]{:S(2)}) collective-permute-start(bf16[1024,640]{1,0:T(8,128)(2,1)S(1)} %copy-done.7), channel_id=1, source_target_pairs={{0,2},{1,3},{2,0},{3,1},{4,6},{5,7},{6,4},{7,5},{8,10},{9,11},{10,... | collective-permute-start | bytes 3932168 | tf_op jit(solution)/shard_map/ppermute | solution.py:459
  187.9 69.7 %collective-permute-start.3 = (bf16[1024,640]{1,0:T(8,128)(2,1)S(1)}, bf16[1024,640]{1,0:T(8,128)(2,1)}, u32[]{:S(2)}, u32[]{:S(2)}) collective-permute-start(bf16[1024,640]{1,0:T(8,128)(2,1)S(1)} %copy-done.7), channel_id=1, source_target_pairs={{0,1},{1,0},{2,3},{3,2},{4,5},{5,4},{6,7},{7,6},{8,9},{9,8},{10,11... | collective-permute-start | bytes 3932168 | tf_op jit(solution)/shard_map/ppermute | solution.py:459
  187.9 55.1 %copy-start.1 = (bf16[2,8,96,640]{3,2,1,0:T(8,128)(2,1)S(1)}, bf16[2,8,96,640]{3,2,1,0:T(8,128)(2,1)}, u32[]{:S(2)}) copy-start(bf16[2,8,96,640]{3,2,1,0:T(8,128)(2,1)} %get-tuple-element.101) | copy-start | bytes 5898244
  196.5 11.9 %collective-permute-start.30 = (bf16[4,80,640]{2,1,0:T(8,128)(2,1)}, bf16[4,80,640]{2,1,0:T(8,128)(2,1)}, u32[]{:S(2)}, u32[]{:S(2)}) collective-permute-start(bf16[4,80,640]{2,1,0:T(8,128)(2,1)} %get-tuple-element.153), channel_id=1, source_target_pairs={{0,4},{1,5},{2,6},{3,7},{4,0},{5,1},{6,2},{7,3},{8,12},{9,13},{10,... | collective-permute-start | bytes 1228808 | tf_op jit(solution)/shard_map/ppermute | solution.py:459
  204.7 36.8 %collective-permute-start.21 = (bf16[4,80,640]{2,1,0:T(8,128)(2,1)}, bf16[4,80,640]{2,1,0:T(8,128)(2,1)}, u32[]{:S(2)}, u32[]{:S(2)}) collective-permute-start(bf16[4,80,640]{2,1,0:T(8,128)(2,1)} %get-tuple-element.155), channel_id=1, source_target_pairs={{0,6},{1,7},{2,4},{3,5},{4,2},{5,3},{6,0},{7,1},{8,14},{9,15},{10,... | collective-permute-start | bytes 1228808 | tf_op jit(solution)/shard_map/ppermute | solution.py:459
  208.4 40.9 %collective-permute-start.22 = (bf16[4,80,640]{2,1,0:T(8,128)(2,1)}, bf16[4,80,640]{2,1,0:T(8,128)(2,1)S(1)}, u32[]{:S(2)}, u32[]{:S(2)}) collective-permute-start(bf16[4,80,640]{2,1,0:T(8,128)(2,1)} %get-tuple-element.157), channel_id=1, source_target_pairs={{0,2},{1,3},{2,0},{3,1},{4,6},{5,7},{6,4},{7,5},{8,10},{9,11},{10,... | collective-permute-start | bytes 1228808 | tf_op jit(solution)/shard_map/ppermute | solution.py:459
  241.5 9.8 %collective-permute-start.23 = (bf16[4,80,640]{2,1,0:T(8,128)(2,1)}, bf16[4,80,640]{2,1,0:T(8,128)(2,1)S(1)}, u32[]{:S(2)}, u32[]{:S(2)}) collective-permute-start(bf16[4,80,640]{2,1,0:T(8,128)(2,1)} %get-tuple-element.156), channel_id=1, source_target_pairs={{0,4},{1,5},{2,6},{3,7},{4,0},{5,1},{6,2},{7,3},{8,12},{9,13},{10,... | collective-permute-start | bytes 1228808 | tf_op jit(solution)/shard_map/ppermute | solution.py:459
  244.7 18.0 %copy-start = (bf16[2,8,80,768]{3,2,1,0:T(8,128)(2,1)S(1)}, bf16[2,8,80,768]{3,2,1,0:T(8,128)(2,1)}, u32[]{:S(2)}) copy-start(bf16[2,8,80,768]{3,2,1,0:T(8,128)(2,1)} %get-tuple-element.99) | copy-start | bytes 5898244
  249.2 10.5 %collective-permute-start.31 = (bf16[80,640]{1,0:T(8,128)(2,1)S(1)}, bf16[80,640]{1,0:T(8,128)(2,1)S(1)}, u32[]{:S(2)}, u32[]{:S(2)}) collective-permute-start(bf16[80,640]{1,0:T(8,128)(2,1)S(1)} %get-tuple-element.140), channel_id=1, source_target_pairs={{0,8},{1,9},{2,10},{3,11},{4,12},{5,13},{6,14},{7,15},{8,0},{9,1},... | collective-permute-start | bytes 307208 | tf_op jit(solution)/shard_map/ppermute | solution.py:459
  251.2 8.8 %collective-permute-start.32 = (bf16[80,640]{1,0:T(8,128)(2,1)S(1)}, bf16[80,640]{1,0:T(8,128)(2,1)S(1)}, u32[]{:S(2)}, u32[]{:S(2)}) collective-permute-start(bf16[80,640]{1,0:T(8,128)(2,1)S(1)} %get-tuple-element.142), channel_id=1, source_target_pairs={{0,16},{1,17},{2,18},{3,19},{4,20},{5,21},{6,22},{7,23},{8,24},{9,... | collective-permute-start | bytes 307208 | tf_op jit(solution)/shard_map/ppermute | solution.py:459
  255.3 21.1 %collective-permute-start.14 = (bf16[4,96,640]{2,1,0:T(8,128)(2,1)S(1)}, bf16[4,96,640]{2,1,0:T(8,128)(2,1)S(1)}, u32[]{:S(2)}, u32[]{:S(2)}) collective-permute-start(bf16[4,96,640]{2,1,0:T(8,128)(2,1)S(1)} %get-tuple-element.146), channel_id=1, source_target_pairs={{0,6},{1,7},{2,4},{3,5},{4,2},{5,3},{6,0},{7,1},{8,14},{9,15},{10,... | collective-permute-start | bytes 1474568 | tf_op jit(solution)/shard_map/ppermute | solution.py:459
  257.5 22.0 %collective-permute-start.15 = (bf16[4,96,640]{2,1,0:T(8,128)(2,1)S(1)}, bf16[4,96,640]{2,1,0:T(8,128)(2,1)S(1)}, u32[]{:S(2)}, u32[]{:S(2)}) collective-permute-start(bf16[4,96,640]{2,1,0:T(8,128)(2,1)S(1)} %get-tuple-element.148), channel_id=1, source_target_pairs={{0,2},{1,3},{2,0},{3,1},{4,6},{5,7},{6,4},{7,5},{8,10},{9,11},{10,... | collective-permute-start | bytes 1474568 | tf_op jit(solution)/shard_map/ppermute | solution.py:459
  258.4 6.6 %collective-permute-start.33 = (bf16[80,640]{1,0:T(8,128)(2,1)S(1)}, bf16[80,640]{1,0:T(8,128)(2,1)S(1)}, u32[]{:S(2)}, u32[]{:S(2)}) collective-permute-start(bf16[80,640]{1,0:T(8,128)(2,1)S(1)} %get-tuple-element.141), channel_id=1, source_target_pairs={{0,24},{1,25},{2,26},{3,27},{4,28},{5,29},{6,30},{7,31},{8,16},{9,... | collective-permute-start | bytes 307208 | tf_op jit(solution)/shard_map/ppermute | solution.py:459
  259.7 6.9 %collective-permute-start.24 = (bf16[80,640]{1,0:T(8,128)(2,1)S(1)}, bf16[80,640]{1,0:T(8,128)(2,1)S(1)}, u32[]{:S(2)}, u32[]{:S(2)}) collective-permute-start(bf16[80,640]{1,0:T(8,128)(2,1)S(1)} %get-tuple-element.143), channel_id=1, source_target_pairs={{0,8},{1,9},{2,10},{3,11},{4,12},{5,13},{6,14},{7,15},{8,0},{9,1},... | collective-permute-start | bytes 307208 | tf_op jit(solution)/shard_map/ppermute | solution.py:459
  260.0 6.6 %collective-permute-start.25 = (bf16[80,640]{1,0:T(8,128)(2,1)S(1)}, bf16[80,640]{1,0:T(8,128)(2,1)S(1)}, u32[]{:S(2)}, u32[]{:S(2)}) collective-permute-start(bf16[80,640]{1,0:T(8,128)(2,1)S(1)} %get-tuple-element.145), channel_id=1, source_target_pairs={{0,16},{1,17},{2,18},{3,19},{4,20},{5,21},{6,22},{7,23},{8,24},{9,... | collective-permute-start | bytes 307208 | tf_op jit(solution)/shard_map/ppermute | solution.py:459
  265.0 60.3 %collective-permute-start.5 = (bf16[1024,640]{1,0:T(8,128)(2,1)}, bf16[1024,640]{1,0:T(8,128)(2,1)S(1)}, u32[]{:S(2)}, u32[]{:S(2)}) collective-permute-start(bf16[1024,640]{1,0:T(8,128)(2,1)} %collective-permute-done.4.refs_2_), channel_id=1, source_target_pairs={{0,1},{1,0},{2,3},{3,2},{4,5},{5,4},{6,7},{7,6},{8,9},{9,8},{10,11... | collective-permute-start | bytes 3932168 | tf_op jit(solution)/shard_map/ppermute | solution.py:459
  266.6 24.7 %collective-permute-start.16 = (bf16[4,96,640]{2,1,0:T(8,128)(2,1)S(1)}, bf16[4,96,640]{2,1,0:T(8,128)(2,1)S(1)}, u32[]{:S(2)}, u32[]{:S(2)}) collective-permute-start(bf16[4,96,640]{2,1,0:T(8,128)(2,1)S(1)} %get-tuple-element.147), channel_id=1, source_target_pairs={{0,4},{1,5},{2,6},{3,7},{4,0},{5,1},{6,2},{7,3},{8,12},{9,13},{10,... | collective-permute-start | bytes 1474568 | tf_op jit(solution)/shard_map/ppermute | solution.py:459
  266.6 6.6 %collective-permute-start.26 = (bf16[80,640]{1,0:T(8,128)(2,1)S(1)}, bf16[80,640]{1,0:T(8,128)(2,1)S(1)}, u32[]{:S(2)}, u32[]{:S(2)}) collective-permute-start(bf16[80,640]{1,0:T(8,128)(2,1)S(1)} %get-tuple-element.144), channel_id=1, source_target_pairs={{0,24},{1,25},{2,26},{3,27},{4,28},{5,29},{6,30},{7,31},{8,16},{9,... | collective-permute-start | bytes 307208 | tf_op jit(solution)/shard_map/ppermute | solution.py:459
  271.5 32.9 %copy-start.11 = (bf16[80,640]{1,0:T(8,128)(2,1)}, bf16[80,640]{1,0:T(8,128)(2,1)S(1)}, u32[]{:S(2)}) copy-start(bf16[80,640]{1,0:T(8,128)(2,1)S(1)} %fusion.36.refs_3_) | copy-start | bytes 307204
  273.1 20.7 %collective-permute-start.7 = (bf16[4,80,768]{2,1,0:T(8,128)(2,1)S(1)}, bf16[4,80,768]{2,1,0:T(8,128)(2,1)S(1)}, u32[]{:S(2)}, u32[]{:S(2)}) collective-permute-start(bf16[4,80,768]{2,1,0:T(8,128)(2,1)S(1)} %get-tuple-element.149), channel_id=1, source_target_pairs={{0,6},{1,7},{2,4},{3,5},{4,2},{5,3},{6,0},{7,1},{8,14},{9,15},{10,... | collective-permute-start | bytes 1474568 | tf_op jit(solution)/shard_map/ppermute | solution.py:459
  276.4 23.0 %collective-permute-start.8 = (bf16[4,80,768]{2,1,0:T(8,128)(2,1)S(1)}, bf16[4,80,768]{2,1,0:T(8,128)(2,1)S(1)}, u32[]{:S(2)}, u32[]{:S(2)}) collective-permute-start(bf16[4,80,768]{2,1,0:T(8,128)(2,1)S(1)} %get-tuple-element.151), channel_id=1, source_target_pairs={{0,2},{1,3},{2,0},{3,1},{4,6},{5,7},{6,4},{7,5},{8,10},{9,11},{10,... | collective-permute-start | bytes 1474568 | tf_op jit(solution)/shard_map/ppermute | solution.py:459
  279.6 21.3 %collective-permute-start.9 = (bf16[4,80,768]{2,1,0:T(8,128)(2,1)S(1)}, bf16[4,80,768]{2,1,0:T(8,128)(2,1)S(1)}, u32[]{:S(2)}, u32[]{:S(2)}) collective-permute-start(bf16[4,80,768]{2,1,0:T(8,128)(2,1)S(1)} %get-tuple-element.150), channel_id=1, source_target_pairs={{0,4},{1,5},{2,6},{3,7},{4,0},{5,1},{6,2},{7,3},{8,12},{9,13},{10,... | collective-permute-start | bytes 1474568 | tf_op jit(solution)/shard_map/ppermute | solution.py:459
  282.6 37.7 %copy-start.12 = (bf16[80,640]{1,0:T(8,128)(2,1)}, bf16[80,640]{1,0:T(8,128)(2,1)S(1)}, u32[]{:S(2)}) copy-start(bf16[80,640]{1,0:T(8,128)(2,1)S(1)} %fusion.43.refs_2_) | copy-start | bytes 307204
  291.3 1.3 collective-permute-start.37
  292.6 19.0 %copy-start.21 = (bf16[80,640]{1,0:T(8,128)(2,1)}, bf16[80,640]{1,0:T(8,128)(2,1)S(1)}, u32[]{:S(2)}) copy-start(bf16[80,640]{1,0:T(8,128)(2,1)S(1)} %collective-permute-done.37.refs_7_) | copy-start | bytes 307204
  292.6 11.8 %collective-permute-start.41 = (bf16[80,640]{1,0:T(8,128)(2,1)S(1)}, bf16[80,640]{1,0:T(8,128)(2,1)S(1)}, u32[]{:S(2)}, u32[]{:S(2)}) collective-permute-start(bf16[80,640]{1,0:T(8,128)(2,1)S(1)} %fusion.36.refs_3_), channel_id=1, source_target_pairs={{0,2},{1,3},{2,0},{3,1},{4,6},{5,7},{6,4},{7,5},{8,10},{9,11},{10,... | collective-permute-start | bytes 307208 | tf_op jit(solution)/shard_map/ppermute | solution.py:459
  293.9 10.6 %collective-permute-start.17 = (bf16[96,640]{1,0:T(8,128)(2,1)S(1)}, bf16[96,640]{1,0:T(8,128)(2,1)S(1)}, u32[]{:S(2)}, u32[]{:S(2)}) collective-permute-start(bf16[96,640]{1,0:T(8,128)(2,1)S(1)} %get-tuple-element.130), channel_id=1, source_target_pairs={{0,8},{1,9},{2,10},{3,11},{4,12},{5,13},{6,14},{7,15},{8,0},{9,1},... | collective-permute-start | bytes 368648 | tf_op jit(solution)/shard_map/ppermute | solution.py:459
  299.3 10.4 %collective-permute-start.18 = (bf16[96,640]{1,0:T(8,128)(2,1)S(1)}, bf16[96,640]{1,0:T(8,128)(2,1)S(1)}, u32[]{:S(2)}, u32[]{:S(2)}) collective-permute-start(bf16[96,640]{1,0:T(8,128)(2,1)S(1)} %get-tuple-element.132), channel_id=1, source_target_pairs={{0,16},{1,17},{2,18},{3,19},{4,20},{5,21},{6,22},{7,23},{8,24},{9,... | collective-permute-start | bytes 368648 | tf_op jit(solution)/shard_map/ppermute | solution.py:459
  300.9 8.9 %collective-permute-start.19 = (bf16[96,640]{1,0:T(8,128)(2,1)S(1)}, bf16[96,640]{1,0:T(8,128)(2,1)S(1)}, u32[]{:S(2)}, u32[]{:S(2)}) collective-permute-start(bf16[96,640]{1,0:T(8,128)(2,1)S(1)} %get-tuple-element.131), channel_id=1, source_target_pairs={{0,24},{1,25},{2,26},{3,27},{4,28},{5,29},{6,30},{7,31},{8,16},{9,... | collective-permute-start | bytes 368648 | tf_op jit(solution)/shard_map/ppermute | solution.py:459
  304.4 31.6 %copy-start.22 = (bf16[80,640]{1,0:T(8,128)(2,1)}, bf16[80,640]{1,0:T(8,128)(2,1)S(1)}, u32[]{:S(2)}) copy-start(bf16[80,640]{1,0:T(8,128)(2,1)S(1)} %collective-permute-done.41.refs_11_) | copy-start | bytes 307204
  304.4 7.2 %collective-permute-start.45 = (bf16[80,640]{1,0:T(8,128)(2,1)S(1)}, bf16[80,640]{1,0:T(8,128)(2,1)S(1)}, u32[]{:S(2)}, u32[]{:S(2)}) collective-permute-start(bf16[80,640]{1,0:T(8,128)(2,1)S(1)} %fusion.36.refs_3_), channel_id=1, source_target_pairs={{0,3},{1,2},{2,1},{3,0},{4,7},{5,6},{6,5},{7,4},{8,11},{9,10},{10,... | collective-permute-start | bytes 307208 | tf_op jit(solution)/shard_map/ppermute | solution.py:459
  304.5 7.7 %collective-permute-start.10 = (bf16[80,768]{1,0:T(8,128)(2,1)S(1)}, bf16[80,768]{1,0:T(8,128)(2,1)S(1)}, u32[]{:S(2)}, u32[]{:S(2)}) collective-permute-start(bf16[80,768]{1,0:T(8,128)(2,1)S(1)} %get-tuple-element.133), channel_id=1, source_target_pairs={{0,8},{1,9},{2,10},{3,11},{4,12},{5,13},{6,14},{7,15},{8,0},{9,1},... | collective-permute-start | bytes 368648 | tf_op jit(solution)/shard_map/ppermute | solution.py:459
  309.8 10.5 %collective-permute-start.11 = (bf16[80,768]{1,0:T(8,128)(2,1)S(1)}, bf16[80,768]{1,0:T(8,128)(2,1)S(1)}, u32[]{:S(2)}, u32[]{:S(2)}) collective-permute-start(bf16[80,768]{1,0:T(8,128)(2,1)S(1)} %get-tuple-element.135), channel_id=1, source_target_pairs={{0,16},{1,17},{2,18},{3,19},{4,20},{5,21},{6,22},{7,23},{8,24},{9,... | collective-permute-start | bytes 368648 | tf_op jit(solution)/shard_map/ppermute | solution.py:459
  309.8 10.5 %collective-permute-start.12 = (bf16[80,768]{1,0:T(8,128)(2,1)S(1)}, bf16[80,768]{1,0:T(8,128)(2,1)S(1)}, u32[]{:S(2)}, u32[]{:S(2)}) collective-permute-start(bf16[80,768]{1,0:T(8,128)(2,1)S(1)} %get-tuple-element.134), channel_id=1, source_target_pairs={{0,24},{1,25},{2,26},{3,27},{4,28},{5,29},{6,30},{7,31},{8,16},{9,... | collective-permute-start | bytes 368648 | tf_op jit(solution)/shard_map/ppermute | solution.py:459
  311.6 24.4 %copy-start.9 = (bf16[96,640]{1,0:T(8,128)(2,1)}, bf16[96,640]{1,0:T(8,128)(2,1)S(1)}, u32[]{:S(2)}) copy-start(bf16[96,640]{1,0:T(8,128)(2,1)S(1)} %fusion.22.refs_1_) | copy-start | bytes 368644
  311.6 24.4 %copy-start.23 = (bf16[80,640]{1,0:T(8,128)(2,1)}, bf16[80,640]{1,0:T(8,128)(2,1)S(1)}, u32[]{:S(2)}) copy-start(bf16[80,640]{1,0:T(8,128)(2,1)S(1)} %collective-permute-done.45.refs_15_) | copy-start | bytes 307204
  311.6 11.1 %collective-permute-start.36 = (bf16[80,640]{1,0:T(8,128)(2,1)S(1)}, bf16[80,640]{1,0:T(8,128)(2,1)S(1)}, u32[]{:S(2)}, u32[]{:S(2)}) collective-permute-start(bf16[80,640]{1,0:T(8,128)(2,1)S(1)} %fusion.43.refs_2_), channel_id=1, source_target_pairs={{0,1},{1,0},{2,3},{3,2},{4,5},{5,4},{6,7},{7,6},{8,9},{9,8},{10,11... | collective-permute-start | bytes 307208 | tf_op jit(solution)/shard_map/ppermute | solution.py:459
  312.2 11.4 %collective-permute-start.40 = (bf16[80,640]{1,0:T(8,128)(2,1)S(1)}, bf16[80,640]{1,0:T(8,128)(2,1)S(1)}, u32[]{:S(2)}, u32[]{:S(2)}) collective-permute-start(bf16[80,640]{1,0:T(8,128)(2,1)S(1)} %fusion.43.refs_2_), channel_id=1, source_target_pairs={{0,2},{1,3},{2,0},{3,1},{4,6},{5,7},{6,4},{7,5},{8,10},{9,11},{10,... | collective-permute-start | bytes 307208 | tf_op jit(solution)/shard_map/ppermute | solution.py:459
  320.3 5.0 %collective-permute-start.44 = (bf16[80,640]{1,0:T(8,128)(2,1)S(1)}, bf16[80,640]{1,0:T(8,128)(2,1)S(1)}, u32[]{:S(2)}, u32[]{:S(2)}) collective-permute-start(bf16[80,640]{1,0:T(8,128)(2,1)S(1)} %fusion.43.refs_2_), channel_id=1, source_target_pairs={{0,3},{1,2},{2,1},{3,0},{4,7},{5,6},{6,5},{7,4},{8,11},{9,10},{10,... | collective-permute-start | bytes 307208 | tf_op jit(solution)/shard_map/ppermute | solution.py:459
  320.3 5.8 %collective-permute-start.35 = (bf16[96,640]{1,0:T(8,128)(2,1)S(1)}, bf16[96,640]{1,0:T(8,128)(2,1)S(1)}, u32[]{:S(2)}, u32[]{:S(2)}) collective-permute-start(bf16[96,640]{1,0:T(8,128)(2,1)S(1)} %fusion.22.refs_1_), channel_id=1, source_target_pairs={{0,1},{1,0},{2,3},{3,2},{4,5},{5,4},{6,7},{7,6},{8,9},{9,8},{10,11... | collective-permute-start | bytes 368648 | tf_op jit(solution)/shard_map/ppermute | solution.py:459
  322.7 13.3 %copy-start.10 = (bf16[80,768]{1,0:T(8,128)(2,1)}, bf16[80,768]{1,0:T(8,128)(2,1)S(1)}, u32[]{:S(2)}) copy-start(bf16[80,768]{1,0:T(8,128)(2,1)S(1)} %fusion.29.refs_0_) | copy-start | bytes 368644
  322.7 13.3 %copy-start.24 = (bf16[80,640]{1,0:T(8,128)(2,1)}, bf16[80,640]{1,0:T(8,128)(2,1)S(1)}, u32[]{:S(2)}) copy-start(bf16[80,640]{1,0:T(8,128)(2,1)S(1)} %collective-permute-done.36.refs_6_) | copy-start | bytes 307204
  322.7 26.1 %collective-permute-start.39 = (bf16[96,640]{1,0:T(8,128)(2,1)S(1)}, bf16[96,640]{1,0:T(8,128)(2,1)S(1)}, u32[]{:S(2)}, u32[]{:S(2)}) collective-permute-start(bf16[96,640]{1,0:T(8,128)(2,1)S(1)} %fusion.22.refs_1_), channel_id=1, source_target_pairs={{0,2},{1,3},{2,0},{3,1},{4,6},{5,7},{6,4},{7,5},{8,10},{9,11},{10,... | collective-permute-start | bytes 368648 | tf_op jit(solution)/shard_map/ppermute | solution.py:459
  323.6 12.4 %copy-start.25 = (bf16[80,640]{1,0:T(8,128)(2,1)}, bf16[80,640]{1,0:T(8,128)(2,1)S(1)}, u32[]{:S(2)}) copy-start(bf16[80,640]{1,0:T(8,128)(2,1)S(1)} %collective-permute-done.40.refs_10_) | copy-start | bytes 307204
  323.6 25.2 %collective-permute-start.43 = (bf16[96,640]{1,0:T(8,128)(2,1)S(1)}, bf16[96,640]{1,0:T(8,128)(2,1)S(1)}, u32[]{:S(2)}, u32[]{:S(2)}) collective-permute-start(bf16[96,640]{1,0:T(8,128)(2,1)S(1)} %fusion.22.refs_1_), channel_id=1, source_target_pairs={{0,3},{1,2},{2,1},{3,0},{4,7},{5,6},{6,5},{7,4},{8,11},{9,10},{10,... | collective-permute-start | bytes 368648 | tf_op jit(solution)/shard_map/ppermute | solution.py:459
  325.3 10.8 %copy-start.26 = (bf16[80,640]{1,0:T(8,128)(2,1)}, bf16[80,640]{1,0:T(8,128)(2,1)S(1)}, u32[]{:S(2)}) copy-start(bf16[80,640]{1,0:T(8,128)(2,1)S(1)} %collective-permute-done.44.refs_14_) | copy-start | bytes 307204
  325.3 23.6 %collective-permute-start.34 = (bf16[80,768]{1,0:T(8,128)(2,1)S(1)}, bf16[80,768]{1,0:T(8,128)(2,1)S(1)}, u32[]{:S(2)}, u32[]{:S(2)}) collective-permute-start(bf16[80,768]{1,0:T(8,128)(2,1)S(1)} %fusion.29.refs_0_), channel_id=1, source_target_pairs={{0,1},{1,0},{2,3},{3,2},{4,5},{5,4},{6,7},{7,6},{8,9},{9,8},{10,11... | collective-permute-start | bytes 368648 | tf_op jit(solution)/shard_map/ppermute | solution.py:459
  325.3 10.8 %copy-start.8 = (bf16[1024,640]{1,0:T(8,128)(2,1)}, bf16[1024,640]{1,0:T(8,128)(2,1)S(1)}, u32[]{:S(2)}) copy-start(bf16[1024,640]{1,0:T(8,128)(2,1)S(1)} %collective-permute-done.5.refs_3_) | copy-start | bytes 3932164
  325.3 23.6 %collective-permute-start.38 = (bf16[80,768]{1,0:T(8,128)(2,1)S(1)}, bf16[80,768]{1,0:T(8,128)(2,1)S(1)}, u32[]{:S(2)}, u32[]{:S(2)}) collective-permute-start(bf16[80,768]{1,0:T(8,128)(2,1)S(1)} %fusion.29.refs_0_), channel_id=1, source_target_pairs={{0,2},{1,3},{2,0},{3,1},{4,6},{5,7},{6,4},{7,5},{8,10},{9,11},{10,... | collective-permute-start | bytes 368648 | tf_op jit(solution)/shard_map/ppermute | solution.py:459
  326.2 9.9 %copy-start.15 = (bf16[96,640]{1,0:T(8,128)(2,1)}, bf16[96,640]{1,0:T(8,128)(2,1)S(1)}, u32[]{:S(2)}) copy-start(bf16[96,640]{1,0:T(8,128)(2,1)S(1)} %collective-permute-done.35.refs_5_) | copy-start | bytes 368644
  326.2 22.7 %collective-permute-start.42 = (bf16[80,768]{1,0:T(8,128)(2,1)S(1)}, bf16[80,768]{1,0:T(8,128)(2,1)S(1)}, u32[]{:S(2)}, u32[]{:S(2)}) collective-permute-start(bf16[80,768]{1,0:T(8,128)(2,1)S(1)} %fusion.29.refs_0_), channel_id=1, source_target_pairs={{0,3},{1,2},{2,1},{3,0},{4,7},{5,6},{6,5},{7,4},{8,11},{9,10},{10,... | collective-permute-start | bytes 368648 | tf_op jit(solution)/shard_map/ppermute | solution.py:459
  (17 other events, 47.0 us)
